TPU v7x, 256 devices: a whole 4x4x8 slice. The times are simulated.
256 devices in a mesh: inst: 32 (over x, z_lo, core), tp: 8 (over z_hi, y).
Axes of the slice: x: 4, y: 4, z: 8 (z_hi: 2, z_lo: 4; z = z_hi * 4 + z_lo), core: 2. Of those that a mesh axis runs over, the one named last changes fastest.
Arguments:
- keys_cache: bfloat16 [32, 4, 1024, 8, 128], P('inst', None, None, 'tp'), may hold values from -4 to 4
- values_cache: bfloat16 [32, 4, 1024, 8, 128], P('inst', None, None, 'tp'), may hold values from -4 to 4
- queries: bfloat16 [4, 64, 8192], P(None, 'inst', 'tp'), may hold values from -9 to 9
- fresh_keys: bfloat16 [4, 64, 1024], P(None, 'inst', 'tp'), may hold values from -6 to 6
- fresh_values: bfloat16 [4, 64, 1024], P(None, 'inst', 'tp'), may hold values from -6 to 6
- out_weight: bfloat16 [8192, 4096], P('tp'), may hold values from -0.5 to 0.5
- partner: int32 [16], replicated, may hold values from 0 to 15, each once
- chosen: int32 [16, 4], replicated, may hold values from 0 to 1, as said below
- lengths: int32 [16, 4], replicated, may hold values from 2 to 2048, as said below
- dest_slot: int32 [16, 4], replicated, may hold values from 0 to 3, each once within a row
Outputs:
- moved_keys: bfloat16 [32, 4, 1024, 8, 128], P('inst', None, None, 'tp')
- moved_values: bfloat16 [32, 4, 1024, 8, 128], P('inst', None, None, 'tp')
- mixed: bfloat16 [4, 64, 4096], P(None, 'inst', 'tp')
Inputs may be any that keep to these rules, and one draw needn't show every extreme that they name: `partner`: a permutation of the 16 instances. `chosen`: each instance hands over one or two requests; in every draw some instance hands over exactly 2. `lengths`: in every instance some request has exactly 2048 positions. `dest_slot`: each row is a permutation of the 4 slots.
All inputs are finite; a program needn't handle non-finite values.
Results may differ from a plain program's by a relative error of at most 0.0056.
Values may be sent and summed in bfloat16 or wider, within the bound.
A program may use at most 64 MiB of HBM per device.

v0:
```python
import jax
import jax.numpy as jnp
from jax import lax
from jax.sharding import PartitionSpec as P

big_negative = -1e30


def swapped(block, axis, distance):
    count = lax.axis_size(axis)
    route = []
    for low in range(count):
        high = low | 1 << distance
        if high != low and high < count:
            route += [(low, high), (high, low)]
    return lax.ppermute(block, axis, route)


def half_partial(block_keys, block_values, asking, span_len, offset):
    scaling = block_keys.shape[3] ** (-0.5)
    scores = (
        jnp.einsum("rkqd,rpkd->rkqp", asking, block_keys, preferred_element_type=jnp.float32)
        * scaling
    )
    places = offset + jnp.arange(block_keys.shape[1], dtype=jnp.int32)
    usable = (places[None, :] < span_len[:, None])[:, None, None, :]
    highest = jnp.max(jnp.where(usable, scores, big_negative), axis=3)
    weights = jnp.where(usable, jnp.exp(scores - highest[..., None]), 0.0)
    totals = jnp.sum(weights, axis=3)
    summed = jnp.einsum(
        "rkqp,rpkd->rkqd",
        weights.astype(jnp.bfloat16),
        block_values,
        preferred_element_type=jnp.float32,
    )
    return (summed, highest, totals)


def combine(first_half, second_half, asking, fresh_key, fresh_value, new_count):
    scaling = asking.shape[3] ** (-0.5)
    scores = (
        jnp.einsum("rkqd,mrkd->rkqm", asking, fresh_key, preferred_element_type=jnp.float32)
        * scaling
    )
    query_rows = asking.shape[2]
    group_size = query_rows // new_count
    causal = (jnp.arange(query_rows, dtype=jnp.int32) // group_size)[:, None] >= jnp.arange(
        new_count, dtype=jnp.int32
    )[None, :]
    highest_new = jnp.max(jnp.where(causal, scores, big_negative), axis=3)
    ceiling = jnp.maximum(jnp.maximum(first_half[1], second_half[1]), highest_new)
    scale_first = jnp.exp(first_half[1] - ceiling)
    scale_second = jnp.exp(second_half[1] - ceiling)
    weights = jnp.where(causal, jnp.exp(scores - ceiling[..., None]), 0.0)
    totals = first_half[2] * scale_first + second_half[2] * scale_second + jnp.sum(weights, axis=3)
    summed = first_half[0] * scale_first[..., None] + second_half[0] * scale_second[..., None]
    summed = summed + jnp.einsum(
        "rkqm,mrkd->rkqd", weights, fresh_value.astype(jnp.float32), precision=lax.Precision.HIGHEST
    )
    head_out = (summed / totals[..., None]).astype(jnp.bfloat16)
    row_count = head_out.shape[0]
    kv_count = head_out.shape[1]
    head_out = head_out.reshape(row_count, kv_count, new_count, group_size, head_out.shape[3])
    return head_out.transpose(2, 0, 1, 3, 4).reshape(
        new_count, row_count, kv_count * group_size * asking.shape[3]
    )


def pick_rows(picked, from_item, fresh_part, old_part):
    new_shape = (picked.shape[0],) + (1,) * (old_part.ndim - 1)
    return jnp.where(picked.reshape(new_shape), jnp.take(fresh_part, from_item, axis=0), old_part)


def on_device(
    keys_cache,
    values_cache,
    queries,
    fresh_keys,
    fresh_values,
    out_weight,
    partner,
    chosen,
    lengths,
    dest_slot,
):
    holders = lax.axis_size("inst")
    holder_index = lax.axis_index("inst")
    instance = holder_index // 2
    my_half = holder_index % 2
    slot_count = keys_cache.shape[1]
    positions = keys_cache.shape[2]
    kv_local = keys_cache.shape[3]
    head_dim = keys_cache.shape[4]
    new_count = queries.shape[0]
    own_rows = queries.shape[1]
    group_size = queries.shape[2] // (kv_local * head_dim)
    pair_count = holders // 2
    inst_ids = jnp.arange(pair_count, dtype=jnp.int32)
    slot_ids = jnp.arange(slot_count, dtype=jnp.int32)
    source_of = jnp.sum(
        jnp.where(partner[None, :] == inst_ids[:, None], inst_ids[None, :], 0), axis=1
    )
    sender = source_of[instance]
    outgoing = (keys_cache[0], values_cache[0])
    spread = (
        lax.all_to_all(outgoing[0], "inst", split_axis=1, concat_axis=1, tiled=True),
        lax.all_to_all(outgoing[1], "inst", split_axis=1, concat_axis=1, tiled=True),
    )
    holder_ids = jnp.arange(holders, dtype=jnp.int32)
    anchor_holder = 2 * jnp.take(source_of, holder_ids // 2) + holder_ids % 2

    def regroup(stacked):
        item_count = stacked.shape[0]
        pieces = stacked.reshape(item_count, holders, positions // holders, kv_local, head_dim)
        return jnp.take(pieces, anchor_holder, axis=1).reshape(stacked.shape)

    relayed = (
        lax.all_to_all(regroup(spread[0]), "inst", split_axis=1, concat_axis=1, tiled=True),
        lax.all_to_all(regroup(spread[1]), "inst", split_axis=1, concat_axis=1, tiled=True),
    )
    usable = jnp.take(chosen[sender], slot_ids) == 1
    target = jnp.take(dest_slot[sender], slot_ids)
    matches = usable[:, None] & (target[:, None] == slot_ids[None, :])
    arrived = jnp.any(matches, axis=0)
    item_ids = jnp.arange(matches.shape[0], dtype=jnp.int32)
    from_item = jnp.sum(jnp.where(matches, item_ids[:, None], 0), axis=0)
    arrived_spans = jnp.take(lengths[sender], slot_ids)
    spans_all = jnp.where(arrived, jnp.take(arrived_spans, from_item), lengths[instance])
    moved_keys = pick_rows(arrived, from_item, relayed[0], keys_cache[0])
    moved_values = pick_rows(arrived, from_item, relayed[1], values_cache[0])
    partner_rows = swapped(queries, "inst", 0)
    lower_rows = jnp.where(my_half == 0, queries, partner_rows)
    upper_rows = jnp.where(my_half == 0, partner_rows, queries)
    all_rows = jnp.concatenate([lower_rows, upper_rows], axis=1)
    asking = all_rows.reshape(new_count, slot_count, kv_local, group_size, head_dim)
    asking = asking.transpose(1, 2, 0, 3, 4).reshape(
        slot_count, kv_local, new_count * group_size, head_dim
    )
    offset = my_half * positions
    local_part = half_partial(moved_keys, moved_values, asking, spans_all, offset)
    kept_part = tuple(
        (lax.dynamic_slice_in_dim(member, my_half * own_rows, own_rows, 0) for member in local_part)
    )
    theirs = tuple(
        (
            lax.dynamic_slice_in_dim(member, (1 - my_half) * own_rows, own_rows, 0)
            for member in local_part
        )
    )
    received = swapped((theirs[0], theirs[1], theirs[2]), "inst", 0)
    lower_first = my_half == 0
    first_half = tuple(
        (
            jnp.where(lower_first, kept_piece, other_piece)
            for kept_piece, other_piece in zip(kept_part, received)
        )
    )
    second_half = tuple(
        (
            jnp.where(lower_first, other_piece, kept_piece)
            for kept_piece, other_piece in zip(kept_part, received)
        )
    )
    own_asking = lax.dynamic_slice_in_dim(asking, my_half * own_rows, own_rows, 0)
    fresh_key = fresh_keys.reshape(new_count, own_rows, kv_local, head_dim)
    fresh_value = fresh_values.reshape(new_count, own_rows, kv_local, head_dim)
    head_out = combine(first_half, second_half, own_asking, fresh_key, fresh_value, new_count)
    partial_out = jnp.einsum(
        "nrh,ho->nro", head_out, out_weight, preferred_element_type=jnp.float32
    )
    mixed = lax.psum_scatter(partial_out, "tp", scatter_dimension=2, tiled=True).astype(
        jnp.bfloat16
    )
    return (moved_keys[None], moved_values[None], mixed)


def solution(mesh):
    in_specs = (
        P("inst", None, None, "tp", None),
        P("inst", None, None, "tp", None),
        P(None, "inst", "tp"),
        P(None, "inst", "tp"),
        P(None, "inst", "tp"),
        P("tp", None),
        P(),
        P(),
        P(),
        P(),
    )
    out_specs = (
        P("inst", None, None, "tp", None),
        P("inst", None, None, "tp", None),
        P(None, "inst", "tp"),
    )
    return jax.shard_map(
        on_device, mesh=mesh, in_specs=in_specs, out_specs=out_specs, check_vma=False
    )
```

profile of v0, /device:TPU:1, one launch (start us, length us, event | category | flops | bytes accessed | tf_op | source)
XLA Modules:
  0.0 269.0 jit_solution(4136992623540883177)
XLA Ops:
  7.2 3.0 %copy.52 = bf16[4,1024,1,128]{3,0,2,1:T(4,128)(2,1)} copy(bf16[4,1024,1,128]{3,1,0,2:T(8,128)(2,1)} %bitcast.150) | data formatting | bytes 2097152 | tf_op jit(solution)/shard_map/squeeze | solution.py:104
  10.2 10.0 %all-to-all-start.2 = ((bf16[4,1024,1,128]{3,0,2,1:T(4,128)(2,1)}), bf16[4,1024,1,128]{3,0,2,1:T(4,128)(2,1)S(1)}, u32[]{:S(2)}, u32[]{:S(2)}) async-start(bf16[4,1024,1,128]{3,0,2,1:T(4,128)(2,1)} %copy.52), calls=%async_computation.2 | async-start | bytes 2097152 | tf_op jit(solution)/shard_map/all_to_all | solution.py:107
  20.2 3.0 %copy.47 = bf16[4,1024,1,128]{3,0,2,1:T(4,128)(2,1)} copy(bf16[4,1024,1,128]{3,1,0,2:T(8,128)(2,1)} %bitcast.151) | data formatting | bytes 2097152 | tf_op jit(solution)/shard_map/squeeze | solution.py:104
  23.2 24.9 %all-to-all-done.2 = bf16[4,1024,1,128]{3,0,2,1:T(4,128)(2,1)S(1)} async-done(((bf16[4,1024,1,128]{3,0,2,1:T(4,128)(2,1)}), bf16[4,1024,1,128]{3,0,2,1:T(4,128)(2,1)S(1)}, u32[]{:S(2)}, u32[]{:S(2)}) %all-to-all-start.2) | async-done | bytes 1048608 | tf_op jit(solution)/shard_map/all_to_all | solution.py:107
  48.1 3.9 %all-to-all-start = ((bf16[4,1024,1,128]{3,0,2,1:T(4,128)(2,1)}), bf16[4,1024,1,128]{3,0,2,1:T(4,128)(2,1)S(1)}, u32[]{:S(2)}, u32[]{:S(2)}) async-start(bf16[4,1024,1,128]{3,0,2,1:T(4,128)(2,1)} %copy.47), calls=%async_computation | async-start | bytes 2097152 | tf_op jit(solution)/shard_map/all_to_all | solution.py:106
  52.2 0.7 gather_fusion
  52.9 0.1 copy.53
  53.1 0.7 gather_fusion.5
  53.8 26.2 %all-to-all-done = bf16[4,1024,1,128]{3,0,2,1:T(4,128)(2,1)S(1)} async-done(((bf16[4,1024,1,128]{3,0,2,1:T(4,128)(2,1)}), bf16[4,1024,1,128]{3,0,2,1:T(4,128)(2,1)S(1)}, u32[]{:S(2)}, u32[]{:S(2)}) %all-to-all-start) | async-done | bytes 1048608 | tf_op jit(solution)/shard_map/all_to_all | solution.py:106
  80.0 0.1 copy.48
  80.1 0.7 gather_fusion.3
  80.9 0.3 bitcast_select_fusion
  81.3 1.8 copy.55
  83.1 3.9 %all-to-all-start.3 = ((bf16[4,1024,1,128]{3,0,2,1:T(4,128)(2,1)}), bf16[4,1024,1,128]{3,0,2,1:T(4,128)(2,1)S(1)}, u32[]{:S(2)}, u32[]{:S(2)}) async-start(bf16[4,1024,1,128]{3,0,2,1:T(4,128)(2,1)} %copy.55), calls=%async_computation.3 | async-start | bytes 2097152 | tf_op jit(solution)/shard_map/all_to_all | solution.py:119
  87.0 0.4 collective-permute-start
  87.4 0.6 dynamic_slice.36
  90.0 0.2 fusion.26
  90.2 0.6 gather_fusion.2
  90.9 0.6 gather_fusion.1
  91.7 1.8 copy.50
  93.5 21.5 %all-to-all-done.3 = bf16[4,1024,1,128]{3,0,2,1:T(4,128)(2,1)S(1)} async-done(((bf16[4,1024,1,128]{3,0,2,1:T(4,128)(2,1)}), bf16[4,1024,1,128]{3,0,2,1:T(4,128)(2,1)S(1)}, u32[]{:S(2)}, u32[]{:S(2)}) %all-to-all-start.3) | async-done | bytes 1048608 | tf_op jit(solution)/shard_map/all_to_all | solution.py:119
  115.0 3.9 %all-to-all-start.1 = ((bf16[4,1024,1,128]{3,0,2,1:T(4,128)(2,1)}), bf16[4,1024,1,128]{3,0,2,1:T(4,128)(2,1)S(1)}, u32[]{:S(2)}, u32[]{:S(2)}) async-start(bf16[4,1024,1,128]{3,0,2,1:T(4,128)(2,1)} %copy.50), calls=%async_computation.1 | async-start | bytes 2097152 | tf_op jit(solution)/shard_map/all_to_all | solution.py:118
  119.0 0.2 fusion.28
  119.2 0.6 gather_fusion.7
  119.8 0.6 gather_fusion.8
  120.8 0.1 select_reduce_fusion.2
  121.0 0.1 copy.80
  121.1 1.7 gather_fusion.6
  122.8 24.1 %all-to-all-done.1 = bf16[4,1024,1,128]{3,0,2,1:T(4,128)(2,1)S(1)} async-done(((bf16[4,1024,1,128]{3,0,2,1:T(4,128)(2,1)}), bf16[4,1024,1,128]{3,0,2,1:T(4,128)(2,1)S(1)}, u32[]{:S(2)}, u32[]{:S(2)}) %all-to-all-start.1) | async-done | bytes 1048608 | tf_op jit(solution)/shard_map/all_to_all | solution.py:118
  146.9 0.1 copy.81
  147.0 0.7 gather_fusion.4
  147.8 2.3 fusion.5
  150.1 0.5 select_reduce_fusion
  150.6 0.2 fusion.7
  150.9 0.3 fusion.2
  151.2 0.4 collective-permute-start.3
  151.6 0.2 collective-permute-start.2
  151.8 0.3 collective-permute-start.1
  152.2 0.6 collective-permute-done.2
  152.9 0.2 collective-permute-done.1
  153.0 0.2 fusion.23
  153.3 4.6 %fusion = f32[4,2,4096]{2,0,1:T(4,128)S(1)} fusion(bf16[4,2,1024]{2,0,1:T(4,128)(2,1)S(1)} %reshape.233, bf16[1024,4096]{1,0:T(8,128)(2,1)} %param.21), kind=kOutput, calls=%fused_computation.9 | convolution fusion | flops 67108864 | bytes 8536064 | tf_op jit(solution)/shard_map/nrh,ho->nro/dot_general | solution.py:168
  157.9 4.4 %copy.63 = f32[4,2,4096]{0,1,2:T(2,128)} copy(f32[4,2,4096]{2,0,1:T(4,128)S(1)} %fusion) | data formatting | bytes 262144
  162.3 5.4 %reshape.347 = f32[4096,8]{1,0:T(8,128)} reshape(f32[4096,2,4]{2,1,0:T(2,128)} %bitcast.141) | data formatting | bytes 262144
  167.8 92.4 %reduce-scatter.4.cloned.1.call-done = f32[512,8]{1,0:T(8,128)} async-done(((f32[4096,8]{1,0:T(8,128)}), f32[512,8]{1,0:T(8,128)}) %reduce-scatter.4.cloned.1.call-update) | async-done | bytes 16400
  260.2 1.1 reshape.348
  261.4 0.1 copy.64
  261.5 0.6 copy.62
  (55 shorter events, 0.9 us)
Async XLA Ops:
  7.2 145.9 %copy-start = (bf16[4,2,128]{2,1,0:T(2,128)(2,1)S(1)}, bf16[4,2,128]{2,1,0:T(2,128)(2,1)}, u32[]{:S(2)}) copy-start(bf16[4,2,128]{2,1,0:T(2,128)(2,1)} %param.20) | copy-start | bytes 6148
  7.2 44.9 %copy-start.8 = (s32[16]{0:T(128)S(1)}, s32[16]{0:T(128)}, u32[]{:S(2)}) copy-start(s32[16]{0:T(128)} %param.22) | copy-start | bytes 196
  10.2 37.9 %all-to-all-start.2 = ((bf16[4,1024,1,128]{3,0,2,1:T(4,128)(2,1)}), bf16[4,1024,1,128]{3,0,2,1:T(4,128)(2,1)S(1)}, u32[]{:S(2)}, u32[]{:S(2)}) async-start(bf16[4,1024,1,128]{3,0,2,1:T(4,128)(2,1)} %copy.52), calls=%async_computation.2 | async-start | bytes 2097152 | tf_op jit(solution)/shard_map/all_to_all | solution.py:107
  48.1 31.9 %all-to-all-start = ((bf16[4,1024,1,128]{3,0,2,1:T(4,128)(2,1)}), bf16[4,1024,1,128]{3,0,2,1:T(4,128)(2,1)S(1)}, u32[]{:S(2)}, u32[]{:S(2)}) async-start(bf16[4,1024,1,128]{3,0,2,1:T(4,128)(2,1)} %copy.47), calls=%async_computation | async-start | bytes 2097152 | tf_op jit(solution)/shard_map/all_to_all | solution.py:106
  53.0 33.9 %copy-start.3 = (bf16[4,2,1024]{2,1,0:T(2,128)(2,1)S(1)}, bf16[4,2,1024]{2,1,0:T(2,128)(2,1)}, u32[]{:S(2)}) copy-start(bf16[4,2,1024]{2,1,0:T(2,128)(2,1)} %param.18) | copy-start | bytes 49156
  53.1 36.9 %copy-start.5 = (s32[16,4]{0,1:T(4,128)S(1)}, s32[16,4]{0,1:T(4,128)}, u32[]{:S(2)}) copy-start(s32[16,4]{0,1:T(4,128)} %param.23) | copy-start | bytes 772
  53.1 36.9 %copy-start.6 = (s32[16,4]{0,1:T(4,128)S(1)}, s32[16,4]{0,1:T(4,128)}, u32[]{:S(2)}) copy-start(s32[16,4]{0,1:T(4,128)} %param.25) | copy-start | bytes 772
  80.9 38.1 %copy-start.4 = (s32[16,4]{0,1:T(4,128)S(1)}, s32[16,4]{0,1:T(4,128)}, u32[]{:S(2)}) copy-start(s32[16,4]{0,1:T(4,128)} %param.24) | copy-start | bytes 772
  81.2 39.6 %copy-start.7 = (bf16[4,2,128]{2,1,0:T(2,128)(2,1)S(1)}, bf16[4,2,128]{2,1,0:T(2,128)(2,1)}, u32[]{:S(2)}) copy-start(bf16[4,2,128]{2,1,0:T(2,128)(2,1)} %param.19) | copy-start | bytes 6148
  83.1 31.9 %all-to-all-start.3 = ((bf16[4,1024,1,128]{3,0,2,1:T(4,128)(2,1)}), bf16[4,1024,1,128]{3,0,2,1:T(4,128)(2,1)S(1)}, u32[]{:S(2)}, u32[]{:S(2)}) async-start(bf16[4,1024,1,128]{3,0,2,1:T(4,128)(2,1)} %copy.55), calls=%async_computation.3 | async-start | bytes 2097152 | tf_op jit(solution)/shard_map/all_to_all | solution.py:119
  87.0 33.7 %collective-permute-start = (bf16[4,2,1024]{2,1,0:T(2,128)(2,1)S(1)}, bf16[4,2,1024]{2,1,0:T(2,128)(2,1)S(1)}, u32[]{:S(2)}, u32[]{:S(2)}) collective-permute-start(bf16[4,2,1024]{2,1,0:T(2,128)(2,1)S(1)} %copy-done.3), channel_id=1, source_target_pairs={{0,8},{8,0},{16,24},{24,16},{32,40},{40,32},{48,56},{56,48},{64,72... | collective-permute-start | bytes 49160 | tf_op jit(solution)/shard_map/ppermute | solution.py:16
  115.0 31.9 %all-to-all-start.1 = ((bf16[4,1024,1,128]{3,0,2,1:T(4,128)(2,1)}), bf16[4,1024,1,128]{3,0,2,1:T(4,128)(2,1)S(1)}, u32[]{:S(2)}, u32[]{:S(2)}) async-start(bf16[4,1024,1,128]{3,0,2,1:T(4,128)(2,1)} %copy.50), calls=%async_computation.1 | async-start | bytes 2097152 | tf_op jit(solution)/shard_map/all_to_all | solution.py:118
  118.9 141.3 %reduce-scatter.4.cloned.1.call-start = ((), (), s32[]{:S(2)}) async-start(), calls=%async_computation.5 | async-start | bytes 2359296
  150.0 12.3 %copy-start.1 = (bf16[4,1024,1,128]{3,1,0,2:T(8,128)(2,1)}, bf16[4,1024,1,128]{3,1,0,2:T(8,128)(2,1)S(1)}, u32[]{:S(2)}) copy-start(bf16[4,1024,1,128]{3,1,0,2:T(8,128)(2,1)S(1)} %get-tuple-element.33) | copy-start | bytes 3145732
  150.1 12.3 %copy-start.2 = (bf16[4,1024,1,128]{3,1,0,2:T(8,128)(2,1)}, bf16[4,1024,1,128]{3,1,0,2:T(8,128)(2,1)S(1)}, u32[]{:S(2)}) copy-start(bf16[4,1024,1,128]{3,1,0,2:T(8,128)(2,1)S(1)} %get-tuple-element.34) | copy-start | bytes 3145732
  151.2 1.6 collective-permute-start.3
  151.6 1.1 collective-permute-start.2
  151.8 1.2 collective-permute-start.1
Sparse Core Ops, SparseCore 0:
  167.9 92.2 reduce-scatter.3
where the time goes:
time: 270 us; the launch traced here: 269 us
  waiting for transfers between devices  190 us (70%)
  local copies, waits for them, and re-layouts  30.3 us (11%)
  starting transfers between devices  23.1 us (9%)
  between operations  16.4 us (6%)
  matrix products  5.88 us (2%)
  other arithmetic  3.39 us (1%)
    unnamed x2, waiting for transfers between devices  92.5 us
    all_to_all x1, waiting for transfers between devices, on_device(): lax.all_to_all(outgoing[0], 'inst', split_axis=1, concat_axis=1, tiled=True)  26.2 us
    all_to_all x1, waiting for transfers between devices, on_device(): lax.all_to_all(outgoing[1], 'inst', split_axis=1, concat_axis=1, tiled=True)  24.9 us
    all_to_all x1, waiting for transfers between devices, on_device(): lax.all_to_all(regroup(spread[0]), 'inst', split_axis=1, concat_axis=1, t...  24.1 us
    all_to_all x1, waiting for transfers between devices, on_device(): lax.all_to_all(regroup(spread[1]), 'inst', split_axis=1, concat_axis=1, t...  21.5 us
    unnamed x23, local copies, waits for them, and re-layouts  11.8 us
    all_to_all x1, starting transfers between devices, on_device(): lax.all_to_all(outgoing[1], 'inst', split_axis=1, concat_axis=1, tiled=True)  10 us
    squeeze x2, local copies, waits for them, and re-layouts, on_device(): outgoing = (keys_cache[0], values_cache[0])  6.02 us
  transfers between devices with their start and end apart: 9, of which 7 were waited for; matrix products, arithmetic and copies ran while one was open for 5% of the time, Pallas kernels for 0%

commit v1 on v0

v1 whole, which is shorter than its diff:
```python
import functools

import jax
import jax.numpy as jnp
from jax import lax
from jax.experimental import pallas as pl
from jax.experimental.pallas import tpu as pltpu
from jax.sharding import PartitionSpec as P

MESH = pl.DeviceIdType.MESH
LOW = -1e30
SLOTS = 4
MOST = 2
SIDE = 4
ITEMS = SIDE * MOST
WIDEST = ITEMS * 2
CAPS = (16,)
GROUPS = 4
SKEW = 4
LATER = 4
UP, DOWN, OUT, SEL, SPAN, PICK, NONE, WHICH, TABLE = 0, 16, 32, 40, 44, 48, 50, 51, 64


def where_am_i():
    inst = lax.axis_index("inst")
    chip = inst // 2
    return inst % 2, chip, chip // SIDE, chip % SIDE


def plan_kernel(partner, chosen, lengths, dest, table, count, start):
    _, me, _, z = where_am_i()
    sent = []
    for i in range(16):
        count[i] = 0
    for s in range(16):
        sent.append(sum(chosen[r, s] for r in range(SLOTS)))
        cls = (s % SIDE) * SIDE + partner[s] % SIDE
        count[cls] = count[cls] + sent[s]
    n = [[count[a * SIDE + b] for b in range(SIDE)] for a in range(SIDE)]

    def flip(a, b, down):
        return n[3 - a][3 - b] if down else n[a][b]

    need = 0
    for down in (False, True):
        f = functools.partial(flip, down=down)
        need = functools.reduce(
            jnp.maximum,
            (
                need,
                f(0, 1) + f(0, 2) + f(0, 3),
                f(0, 2) + f(0, 3) + f(1, 2) + f(1, 3),
                f(0, 3) + f(1, 3) + f(2, 3),
            ),
        )
    which, cap = 0, CAPS[0]
    for i in range(1, len(CAPS)):
        which = jnp.where(need > CAPS[i - 1], i, which)
        cap = jnp.where(need > CAPS[i - 1], CAPS[i], cap)
    for down in (False, True):
        f = functools.partial(flip, down=down)
        places = {
            (0, 3): 0,
            (1, 3): f(0, 3),
            (1, 2): f(0, 3) + f(1, 3),
            (0, 2): cap - f(0, 2),
            (0, 1): f(0, 3),
            (2, 3): f(0, 3) + f(1, 3),
        }
        for (a, b), place in places.items():
            start[(3 - a) * SIDE + 3 - b if down else a * SIDE + b] = place
    for a in range(SIDE):
        start[a * SIDE + a] = 0
    for c in range(WIDEST):
        table[UP + c] = jnp.where(z == 0, 0, ITEMS + c)
        table[DOWN + c] = jnp.where(z == SIDE - 1, 0, ITEMS + cap + c)
    for i in range(OUT, TABLE):
        table[i] = 0
    source = 0
    for s in range(16):
        d = partner[s]
        source = jnp.where(d == me, s, source)
        zs, xs = s % SIDE, s // SIDE
        zd, xd = d % SIDE, d // SIDE
        base = start[zs * SIDE + zd]
        start[zs * SIDE + zd] = base + sent[s]
        for j in range(MOST):
            valid = j < sent[s]
            leaves = valid & (zs == z) & (zd != zs)
            place = jnp.where(zd > zs, UP, DOWN) + base + j
            table[jnp.where(leaves, place, NONE)] = xs * MOST + j
            lands = valid & (zd == z)
            kept = jnp.where(zs < z, ITEMS + base + j, ITEMS + cap + base + j)
            kept = jnp.where(zs == z, xs * MOST + j, kept)
            table[jnp.where(lands, OUT + xd * MOST + j, NONE)] = kept
    mine, theirs = 0, 0
    for r in range(SLOTS):
        table[SPAN + r] = lengths[r, me]
    for r in range(SLOTS):
        go = chosen[r, me] == 1
        table[jnp.where(go, PICK + mine, NONE)] = r
        mine = mine + jnp.where(go, 1, 0)
        come = chosen[r, source] == 1
        slot = dest[r, source]
        theirs = theirs + jnp.where(come, 1, 0)
        table[jnp.where(come, SEL + slot, NONE)] = theirs
        table[jnp.where(come, SPAN + slot, NONE)] = lengths[r, source]
    table[WHICH] = which


def main_kernel(
    cap,
    table,
    q_ref,
    fresh_ref,
    k_ref,
    v_ref,
    w_hbm,
    mk_ref,
    mv_ref,
    mix_ref,
    w_buf,
    q_peer,
    x_out,
    x_in,
    pool,
    up_out,
    up_in,
    down_out,
    down_in,
    y_out,
    y_in,
    acc,
    top,
    tot,
    p_out,
    p_in,
    head,
    lhs,
    s_out,
    s_in,
    w_sem,
    q_sem,
    x_send,
    x_recv,
    up_send,
    up_recv,
    down_send,
    down_recv,
    y_send,
    y_recv,
    p_sem,
    s_send,
    s_recv,
):
    groups = x_out.shape[0]
    rows = x_out.shape[4]
    ctx = k_ref.shape[1]
    span = ctx // groups
    tps = s_out.shape[0]
    cols = s_out.shape[2]
    units = groups * cap
    half, chip, x, z = where_am_i()
    inst = lax.axis_index("inst")
    tp = lax.axis_index("tp")
    peer = (inst + 1 - 2 * half, tp)

    def along_x(dx):
        return (((x + dx) % SIDE * SIDE + z) * 2 + half, tp)

    above = (inst + 2, tp)
    below = (inst - 2, tp)

    barrier = pltpu.get_barrier_semaphore()

    def greet(device):
        pl.semaphore_signal(barrier, inc=1, device_id=device, device_id_type=MESH)

    greet(peer)
    for dx in range(1, SIDE):
        greet(along_x(dx))
    for dt in range(1, tps):
        greet((inst, (tp + dt) % tps))

    @pl.when(z < SIDE - 1)
    def _():
        greet(above)

    @pl.when(z > 0)
    def _():
        greet(below)

    w_copy = pltpu.make_async_copy(w_hbm, w_buf, w_sem)
    w_copy.start()

    def stage(g, carry):
        for dx in range(SIDE):
            to = (x + dx) % SIDE
            at = pl.ds(pl.multiple_of((g * SIDE + to) * rows, rows), rows)
            for j in range(MOST):
                slot = table[PICK + j]
                for kv, ref in enumerate((k_ref, v_ref)):
                    piece = ref[slot, at, :]
                    if dx == 0:
                        pool[g, x * MOST + j, kv] = piece
                    else:
                        x_out[g, dx - 1, j, kv] = piece
        return carry

    lax.fori_loop(0, groups, stage, 0)
    peers = 1 + (SIDE - 1) + (tps - 1)
    pl.semaphore_wait(
        barrier, peers + jnp.where(z > 0, 1, 0) + jnp.where(z < SIDE - 1, 1, 0)
    )

    q_copy = pltpu.make_async_remote_copy(
        q_ref, q_peer, q_sem.at[0], q_sem.at[1], device_id=peer, device_id_type=MESH
    )
    q_copy.start()

    def x_copy(g, dx):
        return pltpu.make_async_remote_copy(
            x_out.at[g, dx - 1],
            x_in.at[g, dx - 1],
            x_send.at[g, dx - 1],
            x_recv.at[g, dx - 1],
            device_id=along_x(dx),
            device_id_type=MESH,
        )

    def y_copy(g, dx):
        return pltpu.make_async_remote_copy(
            y_out.at[g, dx - 1],
            y_in.at[g, dx - 1],
            y_send.at[g, dx - 1],
            y_recv.at[g, dx - 1],
            device_id=along_x(dx),
            device_id_type=MESH,
        )

    def up_copy(k):
        return pltpu.make_async_remote_copy(
            up_out.at[k],
            up_in.at[k],
            up_send.at[k],
            up_recv.at[k],
            device_id=above,
            device_id_type=MESH,
        )

    def down_copy(k):
        return pltpu.make_async_remote_copy(
            down_out.at[k],
            down_in.at[k],
            down_send.at[k],
            down_recv.at[k],
            device_id=below,
            device_id_type=MESH,
        )

    def x_start(g, carry):
        for dx in (1, 3, 2):
            x_copy(g, dx).start()
        return carry

    lax.fori_loop(0, groups, x_start, 0)
    q_copy.wait()

    acc[...] = jnp.zeros_like(acc)
    tot[...] = jnp.zeros_like(tot)
    top[...] = jnp.full_like(top, LOW)
    scaling = q_ref.shape[2] ** -0.5

    def attend(g):
        begin = pl.multiple_of(g * span, span)
        at = pl.ds(begin, span)
        spot = half * ctx + begin + lax.broadcasted_iota(jnp.int32, (q_ref.shape[1], span), 1)
        for slot in range(SLOTS):
            own = slot // 2 == half
            asking = jnp.where(own, q_ref[slot % 2], q_peer[slot % 2])
            scores = (
                lax.dot_general(
                    asking,
                    mk_ref[slot, at, :],
                    (((1,), (1,)), ((), ())),
                    preferred_element_type=jnp.float32,
                )
                * scaling
            )
            usable = spot < table[SPAN + slot]
            before = top[slot][:, :1]
            highest = jnp.max(jnp.where(usable, scores, LOW), axis=1, keepdims=True)
            highest = jnp.maximum(highest, before)
            weights = jnp.where(usable, jnp.exp(scores - highest), 0.0)
            shrink = jnp.exp(before - highest)
            total = tot[slot][:, :1] * shrink + jnp.sum(weights, axis=1, keepdims=True)
            summed = jnp.dot(
                weights.astype(jnp.bfloat16),
                mv_ref[slot, at, :],
                preferred_element_type=jnp.float32,
            )
            acc[slot] = acc[slot] * shrink + summed
            top[slot] = jnp.broadcast_to(highest, top.shape[1:])
            tot[slot] = jnp.broadcast_to(total, tot.shape[1:])

    nearest = jnp.minimum(z, SIDE - 1 - z) * SKEW
    farthest = jnp.maximum(z, SIDE - 1 - z) * SKEW + cap - 1

    def on_group(t, late, act):
        g = (t - late) // cap

        @pl.when((t >= late) & ((t - late) % cap == 0) & (g < groups))
        def _():
            act(g)

    def x_arrive(g):
        for dx in range(1, SIDE):
            x_copy(g, dx).wait_recv()
            origin = (x + SIDE - dx) % SIDE
            for j in range(MOST):
                pool[g, origin * MOST + j] = x_in[g, dx - 1, j]

    def y_start(g):
        for dx in (1, 3, 2):
            to = (x + dx) % SIDE
            for j in range(MOST):
                y_out[g, dx - 1, j] = pool[g, table[OUT + to * MOST + j]]
            y_copy(g, dx).start()

    def settle(g):
        for dx in range(SIDE):
            origin = (x + SIDE - dx) % SIDE
            at = pl.ds(pl.multiple_of((g * SIDE + origin) * rows, rows), rows)
            if dx == 0:
                first = pool[g, table[OUT + x * MOST]]
                second = pool[g, table[OUT + x * MOST + 1]]
            else:
                y_copy(g, dx).wait_recv()
                first = y_in[g, dx - 1, 0]
                second = y_in[g, dx - 1, 1]
            for slot in range(SLOTS):
                sel = table[SEL + slot]
                for kv, (ref, out) in enumerate(((k_ref, mk_ref), (v_ref, mv_ref))):
                    piece = jnp.where(sel == 1, first[kv], ref[slot, at, :])
                    out[slot, at, :] = jnp.where(sel == 2, second[kv], piece)
        attend(g)

    def step(t, carry):
        on_group(t, nearest, x_arrive)
        k = t - z * SKEW

        @pl.when((k >= 0) & (k < units))
        def _():
            g, c = k // cap, k % cap

            @pl.when(z > 0)
            def _():
                up_copy(k).wait_recv()
                pool[g, ITEMS + c] = up_in[k]

            @pl.when(z < SIDE - 1)
            def _():
                up_out[k] = pool[g, table[UP + c]]
                up_copy(k).start()

        m = t - (SIDE - 1 - z) * SKEW

        @pl.when((m >= 0) & (m < units))
        def _():
            g, c = m // cap, m % cap

            @pl.when(z < SIDE - 1)
            def _():
                down_copy(m).wait_recv()
                pool[g, ITEMS + cap + c] = down_in[m]

            @pl.when(z > 0)
            def _():
                down_out[m] = pool[g, table[DOWN + c]]
                down_copy(m).start()

        on_group(t, farthest, y_start)
        on_group(t, farthest + LATER, settle)
        return carry

    lax.fori_loop(0, units + (SIDE - 1) * SKEW + LATER, step, 0)

    lane = lax.broadcasted_iota(jnp.int32, top.shape[1:], 1)
    for r in range(2):
        slot = (1 - half) * 2 + r
        p_out[r, 0] = acc[slot]
        p_out[r, 1] = jnp.where(lane < 64, top[slot], tot[slot])
    p_copy = pltpu.make_async_remote_copy(
        p_out, p_in, p_sem.at[0], p_sem.at[1], device_id=peer, device_id_type=MESH
    )
    p_copy.start()
    w_copy.wait()
    p_copy.wait_recv()
    news = fresh_ref.shape[1] // 2
    size = q_ref.shape[1] // news
    token = lax.broadcasted_iota(jnp.int32, (q_ref.shape[1], 1), 0) // size
    for r in range(2):
        slot = half * 2 + r
        top_a, tot_a = top[slot][:, :1], tot[slot][:, :1]
        top_b, tot_b = p_in[r, 1][:, :1], p_in[r, 1][:, 64:65]
        asking = q_ref[r].astype(jnp.float32)
        peak = jnp.maximum(top_a, top_b)
        fresh = []
        for m in range(news):
            score = jnp.sum(asking * fresh_ref[r, m : m + 1, :], axis=1, keepdims=True) * scaling
            score = jnp.where(token >= m, score, LOW)
            fresh.append(score)
            peak = jnp.maximum(peak, score)
        scale_a = jnp.exp(top_a - peak)
        scale_b = jnp.exp(top_b - peak)
        summed = acc[slot] * scale_a + p_in[r, 0] * scale_b
        total = tot_a * scale_a + tot_b * scale_b
        for m in range(news):
            weight = jnp.where(token >= m, jnp.exp(fresh[m] - peak), 0.0)
            total = total + weight
            summed = summed + weight * fresh_ref[r, news + m : news + m + 1, :]
        head[r] = summed / total
    for r in range(2):
        for a in range(size):
            for n in range(news):
                lhs[n * 2 + r : n * 2 + r + 1, a * 128 : (a + 1) * 128] = head[
                    r, n * size + a : n * size + a + 1, :
                ]
    left = lhs[...].astype(jnp.bfloat16)

    def s_copy(dt):
        return pltpu.make_async_remote_copy(
            s_out.at[dt],
            s_in.at[dt],
            s_send.at[dt],
            s_recv.at[dt],
            device_id=(inst, (tp + dt) % tps),
            device_id_type=MESH,
        )

    for dt in list(range(1, tps)) + [0]:
        to = (tp + dt) % tps
        part = jnp.dot(
            left,
            w_buf[:, pl.ds(pl.multiple_of(to * cols, cols), cols)],
            preferred_element_type=jnp.float32,
        )
        s_out[dt] = part
        if dt:
            s_copy(dt).start()
    mixed = s_out[0]
    for dt in range(1, tps):
        s_copy(dt).wait_recv()
        mixed = mixed + s_in[dt]
    mix_ref[...] = mixed.astype(jnp.bfloat16)

    q_done = [p_copy]
    for copy in q_done:
        copy.wait_send()
    for dt in range(1, tps):
        s_copy(dt).wait_send()

    def x_drain(g, carry):
        for dx in range(1, SIDE):
            x_copy(g, dx).wait_send()
            y_copy(g, dx).wait_send()
        return carry

    lax.fori_loop(0, groups, x_drain, 0)

    def z_drain(k, carry):
        @pl.when(z < SIDE - 1)
        def _():
            up_copy(k).wait_send()

        @pl.when(z > 0)
        def _():
            down_copy(k).wait_send()

        return carry

    lax.fori_loop(0, units, z_drain, 0)


def main_call(cap, collective_id, table, asking, fresh, keys, values, weight):
    slots, ctx, dim = keys.shape
    rows = ctx // (GROUPS * SIDE)
    tps = lax.axis_size("tp")
    cols = weight.shape[1] // tps
    queries = asking.shape[1]
    unit = (2, rows, dim)
    units = GROUPS * cap
    bf16, f32 = jnp.bfloat16, jnp.float32
    vmem = pl.BlockSpec(memory_space=pltpu.VMEM)
    spread = pltpu.VMEM((GROUPS, SIDE - 1, MOST) + unit, bf16)
    line = pltpu.VMEM((units,) + unit, bf16)
    dma = pltpu.SemaphoreType.DMA
    return pl.pallas_call(
        functools.partial(main_kernel, cap),
        out_shape=(
            jax.ShapeDtypeStruct(keys.shape, bf16),
            jax.ShapeDtypeStruct(values.shape, bf16),
            jax.ShapeDtypeStruct((asking.shape[0] * fresh.shape[1] // 2, cols), bf16),
        ),
        in_specs=[
            pl.BlockSpec(memory_space=pltpu.SMEM),
            vmem,
            vmem,
            vmem,
            vmem,
            pl.BlockSpec(memory_space=pl.ANY),
        ],
        out_specs=(vmem, vmem, vmem),
        scratch_shapes=[
            pltpu.VMEM(weight.shape, bf16),
            pltpu.VMEM(asking.shape, bf16),
            spread,
            spread,
            pltpu.VMEM((GROUPS, ITEMS + 2 * cap) + unit, bf16),
            line,
            line,
            line,
            line,
            spread,
            spread,
            pltpu.VMEM((slots, queries, dim), f32),
            pltpu.VMEM((slots, queries, dim), f32),
            pltpu.VMEM((slots, queries, dim), f32),
            pltpu.VMEM((2, 2, queries, dim), f32),
            pltpu.VMEM((2, 2, queries, dim), f32),
            pltpu.VMEM((2, queries, dim), f32),
            pltpu.VMEM((8, weight.shape[0]), f32),
            pltpu.VMEM((tps, 8, cols), f32),
            pltpu.VMEM((tps, 8, cols), f32),
            dma,
            dma((2,)),
            dma((GROUPS, SIDE - 1)),
            dma((GROUPS, SIDE - 1)),
            dma((units,)),
            dma((units,)),
            dma((units,)),
            dma((units,)),
            dma((GROUPS, SIDE - 1)),
            dma((GROUPS, SIDE - 1)),
            dma((2,)),
            dma((tps,)),
            dma((tps,)),
        ],
        compiler_params=pltpu.CompilerParams(
            collective_id=collective_id, has_side_effects=True, vmem_limit_bytes=56 << 20
        ),
        name=f"move_attend_{cap}",
    )(table, asking, fresh, keys, values, weight)


def on_device(
    keys_cache,
    values_cache,
    queries,
    fresh_keys,
    fresh_values,
    out_weight,
    partner,
    chosen,
    lengths,
    dest_slot,
):
    _, slots, ctx, _, dim = keys_cache.shape
    news, own = queries.shape[:2]
    size = queries.shape[2] // dim
    smem = pl.BlockSpec(memory_space=pltpu.SMEM)
    table = pl.pallas_call(
        plan_kernel,
        out_shape=jax.ShapeDtypeStruct((TABLE,), jnp.int32),
        in_specs=[smem] * 4,
        out_specs=smem,
        scratch_shapes=[pltpu.SMEM((16,), jnp.int32), pltpu.SMEM((16,), jnp.int32)],
        name="plan",
    )(partner, chosen.T, lengths.T, dest_slot.T)
    asking = queries.reshape(news, own, size, dim).transpose(1, 0, 2, 3)
    asking = asking.reshape(own, news * size, dim)
    fresh = jnp.concatenate([fresh_keys, fresh_values], axis=0).transpose(1, 0, 2)
    fresh = fresh.astype(jnp.float32)
    keys = keys_cache.reshape(slots, ctx, dim)
    values = values_cache.reshape(slots, ctx, dim)
    args = (table, asking, fresh, keys, values, out_weight)
    if len(CAPS) == 1:
        moved_keys, moved_values, mixed = main_call(CAPS[0], 0, *args)
    else:
        moved_keys, moved_values, mixed = lax.switch(
            table[WHICH],
            [functools.partial(main_call, cap, i) for i, cap in enumerate(CAPS)],
            *args,
        )
    return (
        moved_keys.reshape(keys_cache.shape),
        moved_values.reshape(values_cache.shape),
        mixed.reshape(news, own, mixed.shape[1]),
    )


def solution(mesh):
    in_specs = (
        P("inst", None, None, "tp", None),
        P("inst", None, None, "tp", None),
        P(None, "inst", "tp"),
        P(None, "inst", "tp"),
        P(None, "inst", "tp"),
        P("tp", None),
        P(),
        P(),
        P(),
        P(),
    )
    out_specs = (
        P("inst", None, None, "tp", None),
        P("inst", None, None, "tp", None),
        P(None, "inst", "tp"),
    )
    return jax.shard_map(
        on_device, mesh=mesh, in_specs=in_specs, out_specs=out_specs, check_vma=False
    )
```

time: 270 us -> 112 us (0.41)
  waiting for transfers between devices: 190 us -> 0 us
  Pallas kernels: 0 us -> 102 us
  starting transfers between devices: 23.1 us -> 0 us
  local copies, waits for them, and re-layouts: 30.3 us -> 8.54 us
  between operations: 16.4 us -> 0.65 us
  matrix products: 5.88 us -> 0 us
  other arithmetic: 3.39 us -> 0.61 us
    pallas_call x0 -> x2, Pallas kernels: none -> 102 us  [the longest x1 100 us: main_call(): pl.pallas_call(functools.partial(main_kernel, cap), out_shape=(jax.ShapeD...]
    all_to_all x4 -> x0, waiting for transfers between devices: 96.6 us -> none  [the longest x1 26.2 us: on_device(): lax.all_to_all(outgoing[0], 'inst', split_axis=1, concat_axis=1, tiled=True)]
    unnamed x2 -> x0, waiting for transfers between devices: 92.5 us -> none
    all_to_all x4 -> x0, starting transfers between devices: 21.7 us -> none  [the longest x1 10 us: on_device(): lax.all_to_all(outgoing[1], 'inst', split_axis=1, concat_axis=1, tiled=True)]
    gather x9 -> x0, local copies, waits for them, and re-layouts: 7.16 us -> none  [the longest x2 2.4 us: pick_rows(): jnp.take(fresh_part, from_item, axis=0)]
    squeeze x2 -> x0, local copies, waits for them, and re-layouts: 6.02 us -> none  [on_device(): outgoing = (keys_cache[0], values_cache[0])]
    unnamed x23 -> x4, local copies, waits for them, and re-layouts: 11.8 us -> 5.89 us
    dot_general x5 -> x0, matrix products: 5.88 us -> none  [the longest x1 4.63 us: on_device(): jnp.einsum('nrh,ho->nro', head_out, out_weight, preferred_element_type=jn...]
  transfers between devices with their start and end apart: 9 -> 0, of which waited for: 7 -> 0; matrix products, arithmetic and copies ran while one was open for 5% -> 0% of each run, Pallas kernels for 0% -> 0%
where the time goes in v1:
time: 112 us
  Pallas kernels  102 us (91%)
  local copies, waits for them, and re-layouts  8.54 us (8%)
    pallas_call x1, Pallas kernels, main_call(): pl.pallas_call(functools.partial(main_kernel, cap), out_shape=(jax.ShapeD...  100 us
    unnamed x4, local copies, waits for them, and re-layouts  5.89 us

profile of v1, /device:TPU:1, one launch (start us, length us, event | category | flops | bytes accessed | tf_op | source)
XLA Modules:
  0.0 112.1 jit_solution(6712403541104441566)
XLA Ops:
  0.6 1.8 %plan.1.table = s32[64]{0:T(128)} custom-call(s32[16]{0:T(128)} %partner.1, s32[4,16]{1,0:T(4,128)} %bitcast.23, s32[4,16]{1,0:T(4,128)} %bitcast.24, s32[4,16]{1,0:T(4,128)} %bitcast.25), custom_call_target="tpu_custom_call" | custom-call | tf_op jit(solution)/shard_map/plan/pallas_call | solution.py:572
  2.4 0.7 copy.14
  3.1 0.7 copy.15
  3.8 0.6 convert_bitcast_fusion.fresh_ref
  4.4 0.7 reshape.27
  5.2 0.6 copy.19
  5.8 100.5 %move_attend_16.1 = (bf16[4,1024,128]{2,1,0:T(8,128)(2,1)}, bf16[4,1024,128]{2,1,0:T(8,128)(2,1)}, bf16[8,512]{1,0:T(8,128)(2,1)}) custom-call(s32[64]{0:T(128)} %plan.1.table, bf16[2,32,128]{2,1,0:T(8,128)(2,1)} %bitcast.22, f32[2,8,128]{2,1,0:T(8,128)} %convert_bitcast_fusion.fresh_ref, bf16[4,1024,128]{2,1,0:T(8,128)(2,1)} %bitcast.18, ...), custom_call_target="tpu_custom_call" | custom-call | tf_op jit(solution)/shard_map/move_attend_16/pallas_call | solution.py:498
  106.2 1.3 %reshape.33 = bf16[4,2,512]{2,1,0:T(2,128)(2,1)} reshape(bf16[8,512]{1,0:T(8,128)(2,1)} %get-tuple-element.8) | data formatting | bytes 16384 | tf_op jit(solution)/shard_map/reshape | solution.py:598
  107.6 2.3 %copy.22 = bf16[1,4,1024,1,128]{4,2,3,1,0:T(8,128)(2,1)} copy(bf16[1,4,1024,1,128]{4,2,3,1,0:T(8,128)(2,1)} %bitcast.21) | data formatting | bytes 2097152
  109.8 2.3 %copy.23 = bf16[1,4,1024,1,128]{4,2,3,1,0:T(8,128)(2,1)} copy(bf16[1,4,1024,1,128]{4,2,3,1,0:T(8,128)(2,1)} %bitcast.20) | data formatting | bytes 2097152

commit v2 on v1

--- a/solution.py
+++ b/solution.py
@@ -14,7 +14,7 @@
 SIDE = 4
 ITEMS = SIDE * MOST
 WIDEST = ITEMS * 2
-CAPS = (16,)
+CAPS = (5, 6, 7, 8, 10, 16)
 GROUPS = 4
 SKEW = 4
 LATER = 4

time: 112 us -> 75.4 us (0.67)
  Pallas kernels: 102 us -> 68.3 us
  local copies, waits for them, and re-layouts: 8.54 us -> 5.24 us
    pallas_call x1, Pallas kernels: 100 us -> 66.4 us  [main_call(): pl.pallas_call(functools.partial(main_kernel, cap), out_shape=(jax.ShapeD...]
    unnamed x4, local copies, waits for them, and re-layouts: 5.89 us -> 3.31 us
where the time goes in v2:
time: 75.4 us; the launch traced here: 75.2 us
  Pallas kernels  68.3 us (91%)
  local copies, waits for them, and re-layouts  5.24 us (7%)
  between operations  1.31 us (2%)
    pallas_call x1, Pallas kernels, main_call(): pl.pallas_call(functools.partial(main_kernel, cap), out_shape=(jax.ShapeD...  66.4 us
    unnamed x4, local copies, waits for them, and re-layouts  3.31 us
    pallas_call x1, Pallas kernels, on_device(): pl.pallas_call(plan_kernel, out_shape=jax.ShapeDtypeStruct((TABLE,), jnp....  1.89 us

profile of v2, /device:TPU:1, one launch (start us, length us, event | category | flops | bytes accessed | tf_op | source)
XLA Modules:
  0.0 75.2 jit_solution(4527339133370430961)
XLA Ops:
  0.6 1.9 %plan.1 = s32[64]{0:T(128)S(1)} custom-call(s32[16]{0:T(128)} %partner.1, s32[4,16]{1,0:T(4,128)} %bitcast.79, s32[4,16]{1,0:T(4,128)} %bitcast.80, s32[4,16]{1,0:T(4,128)} %bitcast.81), custom_call_target="tpu_custom_call" | custom-call | tf_op jit(solution)/shard_map/plan/pallas_call | solution.py:572
  2.5 0.6 slice.3
  3.8 0.7 copy.14
  4.4 0.7 copy.15
  5.1 0.7 reshape.130
  5.9 66.7 %conditional.1 = ((bf16[4,1024,128]{2,1,0:T(8,128)(2,1)S(1)}, bf16[4,1024,128]{2,1,0:T(8,128)(2,1)S(1)}, bf16[8,512]{1,0:T(8,128)(2,1)S(1)})) conditional(s32[]{:T(128)} %bitcast.45, (bf16[2,4,8,128]{3,2,1,0:T(8,128)(2,1)S(1)}, bf16[1,4,1024,1,128]{4,2,3,1,0:T(8,128)(2,1)}, bf16[1,4,1024,1,128]{4,2,3,1,0:T(8,128)(2,1)}, ...), branch_computations={%region_0.0_spmd, %region_1.0_spmd, %region_2.0_spmd, %region_3.0_... | conditional | bytes 8 | solution.py:590
  5.9 66.4 %move_attend_5.1 = (bf16[4,1024,128]{2,1,0:T(8,128)(2,1)S(1)}, bf16[4,1024,128]{2,1,0:T(8,128)(2,1)S(1)}, bf16[8,512]{1,0:T(8,128)(2,1)S(1)}) custom-call(s32[64]{0:T(128)S(1)} %get-tuple-element.111.table, bf16[2,32,128]{2,1,0:T(8,128)(2,1)S(1)} %bitcast.73, f32[2,8,128]{2,1,0:T(8,128)S(1)} %get-tuple-element.113.fresh_ref, bf16[4,1024,128]{2,1,0:T(8,128)(2,1)} %bitcast.53, ...), custom_call_target="tpu_custom_call" | custom-call | tf_op jit(solution)/shard_map/cond/branch_0_fun/move_attend_5/pallas_call | solution.py:498
  72.6 0.6 reshape.127
  73.2 1.0 %copy.51 = bf16[1,4,1024,1,128]{4,2,3,1,0:T(8,128)(2,1)} copy(bf16[1,4,1024,1,128]{4,2,3,1,0:T(8,128)(2,1)S(1)} %bitcast.65) | data formatting | bytes 2097152
  74.2 1.0 %copy.52 = bf16[1,4,1024,1,128]{4,2,3,1,0:T(8,128)(2,1)} copy(bf16[1,4,1024,1,128]{4,2,3,1,0:T(8,128)(2,1)S(1)} %bitcast.66) | data formatting | bytes 2097152
  (2 shorter events, 0.0 us)

commit v3 on v2

--- a/solution.py
+++ b/solution.py
@@ -16,8 +16,7 @@
 WIDEST = ITEMS * 2
 CAPS = (5, 6, 7, 8, 10, 16)
 GROUPS = 4
-SKEW = 4
-LATER = 4
+SKEW = 6
 UP, DOWN, OUT, SEL, SPAN, PICK, NONE, WHICH, TABLE = 0, 16, 32, 40, 44, 48, 50, 51, 64
 
 
@@ -95,6 +94,7 @@
             table[jnp.where(lands, OUT + xd * MOST + j, NONE)] = kept
     mine, theirs = 0, 0
     for r in range(SLOTS):
+        table[SEL + r] = r
         table[SPAN + r] = lengths[r, me]
     for r in range(SLOTS):
         go = chosen[r, me] == 1
@@ -103,7 +103,7 @@
         come = chosen[r, source] == 1
         slot = dest[r, source]
         theirs = theirs + jnp.where(come, 1, 0)
-        table[jnp.where(come, SEL + slot, NONE)] = theirs
+        table[jnp.where(come, SEL + slot, NONE)] = SLOTS - 1 + theirs
         table[jnp.where(come, SPAN + slot, NONE)] = lengths[r, source]
     table[WHICH] = which
 
@@ -111,15 +111,20 @@
 def main_kernel(
     cap,
     table,
-    q_ref,
-    fresh_ref,
-    k_ref,
-    v_ref,
+    raw_ref,
+    fk_ref,
+    fv_ref,
+    k_hbm,
+    v_hbm,
     w_hbm,
     mk_ref,
     mv_ref,
     mix_ref,
     w_buf,
+    k_ref,
+    v_ref,
+    q_rows,
+    q_ref,
     q_peer,
     x_out,
     x_in,
@@ -140,6 +145,7 @@
     s_out,
     s_in,
     w_sem,
+    kv_sem,
     q_sem,
     x_send,
     x_recv,
@@ -158,8 +164,12 @@
     ctx = k_ref.shape[1]
     span = ctx // groups
     tps = s_out.shape[0]
-    cols = s_out.shape[2]
+    cols = mix_ref.shape[1]
+    wide = cols // 2
     units = groups * cap
+    news, _, width = raw_ref.shape
+    dim = k_ref.shape[2]
+    size = width // dim
     half, chip, x, z = where_am_i()
     inst = lax.axis_index("inst")
     tp = lax.axis_index("tp")
@@ -171,6 +181,10 @@
     above = (inst + 2, tp)
     below = (inst - 2, tp)
 
+    k_copy = pltpu.make_async_copy(k_hbm, k_ref.at[:SLOTS], kv_sem.at[0])
+    v_copy = pltpu.make_async_copy(v_hbm, v_ref.at[:SLOTS], kv_sem.at[1])
+    k_copy.start()
+    v_copy.start()
     barrier = pltpu.get_barrier_semaphore()
 
     def greet(device):
@@ -191,7 +205,8 @@
         greet(below)
 
     w_copy = pltpu.make_async_copy(w_hbm, w_buf, w_sem)
-    w_copy.start()
+    k_copy.wait()
+    v_copy.wait()
 
     def stage(g, carry):
         for dx in range(SIDE):
@@ -207,16 +222,11 @@
                         x_out[g, dx - 1, j, kv] = piece
         return carry
 
-    lax.fori_loop(0, groups, stage, 0)
+    stage(0, 0)
     peers = 1 + (SIDE - 1) + (tps - 1)
     pl.semaphore_wait(
         barrier, peers + jnp.where(z > 0, 1, 0) + jnp.where(z < SIDE - 1, 1, 0)
     )
-
-    q_copy = pltpu.make_async_remote_copy(
-        q_ref, q_peer, q_sem.at[0], q_sem.at[1], device_id=peer, device_id_type=MESH
-    )
-    q_copy.start()
 
     def x_copy(g, dx):
         return pltpu.make_async_remote_copy(
@@ -258,60 +268,81 @@
             device_id_type=MESH,
         )
 
-    def x_start(g, carry):
+    def x_start(g):
         for dx in (1, 3, 2):
             x_copy(g, dx).start()
+
+    x_start(0)
+
+    def x_rest(g, carry):
+        stage(g, carry)
+        x_start(g)
         return carry
 
-    lax.fori_loop(0, groups, x_start, 0)
-    q_copy.wait()
-
+    lax.fori_loop(1, groups, x_rest, 0)
+    w_copy.start()
+    for n in range(news):
+        raw = raw_ref[n].astype(jnp.float32)
+        for r in range(2):
+            for a in range(size):
+                q_rows[r, n * size + a : n * size + a + 1, :] = raw[
+                    r : r + 1, a * dim : (a + 1) * dim
+                ]
+    for r in range(2):
+        q_ref[r] = q_rows[r].astype(jnp.bfloat16)
+    q_copy = pltpu.make_async_remote_copy(
+        q_ref, q_peer, q_sem.at[0], q_sem.at[1], device_id=peer, device_id_type=MESH
+    )
+    q_copy.start()
     acc[...] = jnp.zeros_like(acc)
     tot[...] = jnp.zeros_like(tot)
     top[...] = jnp.full_like(top, LOW)
-    scaling = q_ref.shape[2] ** -0.5
-
-    def attend(g):
+    scaling = dim**-0.5
+    q_copy.wait()
+
+    def attend(g, slot):
         begin = pl.multiple_of(g * span, span)
         at = pl.ds(begin, span)
         spot = half * ctx + begin + lax.broadcasted_iota(jnp.int32, (q_ref.shape[1], span), 1)
-        for slot in range(SLOTS):
-            own = slot // 2 == half
-            asking = jnp.where(own, q_ref[slot % 2], q_peer[slot % 2])
-            scores = (
-                lax.dot_general(
-                    asking,
-                    mk_ref[slot, at, :],
-                    (((1,), (1,)), ((), ())),
-                    preferred_element_type=jnp.float32,
-                )
-                * scaling
-            )
-            usable = spot < table[SPAN + slot]
-            before = top[slot][:, :1]
-            highest = jnp.max(jnp.where(usable, scores, LOW), axis=1, keepdims=True)
-            highest = jnp.maximum(highest, before)
-            weights = jnp.where(usable, jnp.exp(scores - highest), 0.0)
-            shrink = jnp.exp(before - highest)
-            total = tot[slot][:, :1] * shrink + jnp.sum(weights, axis=1, keepdims=True)
-            summed = jnp.dot(
-                weights.astype(jnp.bfloat16),
-                mv_ref[slot, at, :],
+        own = slot // 2 == half
+        source = table[SEL + slot]
+        keys, values = k_ref[source, at, :], v_ref[source, at, :]
+        mk_ref[slot, at, :] = keys
+        mv_ref[slot, at, :] = values
+        asking = jnp.where(own, q_ref[slot % 2], q_peer[slot % 2])
+        scores = (
+            lax.dot_general(
+                asking,
+                keys,
+                (((1,), (1,)), ((), ())),
                 preferred_element_type=jnp.float32,
             )
-            acc[slot] = acc[slot] * shrink + summed
-            top[slot] = jnp.broadcast_to(highest, top.shape[1:])
-            tot[slot] = jnp.broadcast_to(total, tot.shape[1:])
+            * scaling
+        )
+        usable = spot < table[SPAN + slot]
+        before = top[slot][:, :1]
+        highest = jnp.max(jnp.where(usable, scores, LOW), axis=1, keepdims=True)
+        highest = jnp.maximum(highest, before)
+        weights = jnp.where(usable, jnp.exp(scores - highest), 0.0)
+        shrink = jnp.exp(before - highest)
+        total = tot[slot][:, :1] * shrink + jnp.sum(weights, axis=1, keepdims=True)
+        summed = jnp.dot(
+            weights.astype(jnp.bfloat16),
+            values,
+            preferred_element_type=jnp.float32,
+        )
+        acc[slot] = acc[slot] * shrink + summed
+        top[slot] = jnp.broadcast_to(highest, top.shape[1:])
+        tot[slot] = jnp.broadcast_to(total, tot.shape[1:])
 
     nearest = jnp.minimum(z, SIDE - 1 - z) * SKEW
     farthest = jnp.maximum(z, SIDE - 1 - z) * SKEW + cap - 1
 
-    def on_group(t, late, act):
-        g = (t - late) // cap
-
-        @pl.when((t >= late) & ((t - late) % cap == 0) & (g < groups))
-        def _():
-            act(g)
+    factor = -(-(1 << 16) // cap)
+
+    def split(k):
+        g = lax.shift_right_arithmetic(k * factor, 16)
+        return g, k - g * cap
 
     def x_arrive(g):
         for dx in range(1, SIDE):
@@ -331,27 +362,32 @@
         for dx in range(SIDE):
             origin = (x + SIDE - dx) % SIDE
             at = pl.ds(pl.multiple_of((g * SIDE + origin) * rows, rows), rows)
-            if dx == 0:
-                first = pool[g, table[OUT + x * MOST]]
-                second = pool[g, table[OUT + x * MOST + 1]]
-            else:
+            if dx:
                 y_copy(g, dx).wait_recv()
-                first = y_in[g, dx - 1, 0]
-                second = y_in[g, dx - 1, 1]
-            for slot in range(SLOTS):
-                sel = table[SEL + slot]
-                for kv, (ref, out) in enumerate(((k_ref, mk_ref), (v_ref, mv_ref))):
-                    piece = jnp.where(sel == 1, first[kv], ref[slot, at, :])
-                    out[slot, at, :] = jnp.where(sel == 2, second[kv], piece)
-        attend(g)
+            for j in range(MOST):
+                if dx:
+                    piece = y_in[g, dx - 1, j]
+                else:
+                    piece = pool[g, table[OUT + x * MOST + j]]
+                k_ref[SLOTS + j, at, :] = piece[0]
+                v_ref[SLOTS + j, at, :] = piece[1]
 
     def step(t, carry):
-        on_group(t, nearest, x_arrive)
+        early = t - nearest
+
+        @pl.when((early >= 0) & (early < units))
+        def _():
+            g, c = split(early)
+
+            @pl.when(c == 0)
+            def _():
+                x_arrive(g)
+
         k = t - z * SKEW
 
         @pl.when((k >= 0) & (k < units))
         def _():
-            g, c = k // cap, k % cap
+            g, c = split(k)
 
             @pl.when(z > 0)
             def _():
@@ -367,7 +403,7 @@
 
         @pl.when((m >= 0) & (m < units))
         def _():
-            g, c = m // cap, m % cap
+            g, c = split(m)
 
             @pl.when(z < SIDE - 1)
             def _():
@@ -379,11 +415,31 @@
                 down_out[m] = pool[g, table[DOWN + c]]
                 down_copy(m).start()
 
-        on_group(t, farthest, y_start)
-        on_group(t, farthest + LATER, settle)
+        late = t - farthest
+
+        @pl.when(late >= 0)
+        def _():
+            g, c = split(late)
+
+            @pl.when((c == 0) & (g < groups))
+            def _():
+                y_start(g)
+
+            @pl.when((g >= 1) & (g <= groups))
+            def _():
+                @pl.when(c == 0)
+                def _():
+                    settle(g - 1)
+
+                for slot in range(SLOTS):
+
+                    @pl.when(c == slot + 1)
+                    def _():
+                        attend(g - 1, slot)
+
         return carry
 
-    lax.fori_loop(0, units + (SIDE - 1) * SKEW + LATER, step, 0)
+    lax.fori_loop(0, units + (SIDE - 1) * SKEW + cap + SLOTS, step, 0)
 
     lane = lax.broadcasted_iota(jnp.int32, top.shape[1:], 1)
     for r in range(2):
@@ -394,11 +450,32 @@
         p_out, p_in, p_sem.at[0], p_sem.at[1], device_id=peer, device_id_type=MESH
     )
     p_copy.start()
+
+    def x_drain(g, carry):
+        for dx in range(1, SIDE):
+            x_copy(g, dx).wait_send()
+            y_copy(g, dx).wait_send()
+        return carry
+
+    lax.fori_loop(0, groups, x_drain, 0)
+
+    def z_drain(k, carry):
+        @pl.when(z < SIDE - 1)
+        def _():
+            up_copy(k).wait_send()
+
+        @pl.when(z > 0)
+        def _():
+            down_copy(k).wait_send()
+
+        return carry
+
+    lax.fori_loop(0, units, z_drain, 0)
     w_copy.wait()
     p_copy.wait_recv()
-    news = fresh_ref.shape[1] // 2
-    size = q_ref.shape[1] // news
     token = lax.broadcasted_iota(jnp.int32, (q_ref.shape[1], 1), 0) // size
+    fresh_keys = [fk_ref[m].astype(jnp.float32) for m in range(news)]
+    fresh_values = [fv_ref[m].astype(jnp.float32) for m in range(news)]
     for r in range(2):
         slot = half * 2 + r
         top_a, tot_a = top[slot][:, :1], tot[slot][:, :1]
@@ -407,7 +484,7 @@
         peak = jnp.maximum(top_a, top_b)
         fresh = []
         for m in range(news):
-            score = jnp.sum(asking * fresh_ref[r, m : m + 1, :], axis=1, keepdims=True) * scaling
+            score = jnp.sum(asking * fresh_keys[m][r : r + 1], axis=1, keepdims=True) * scaling
             score = jnp.where(token >= m, score, LOW)
             fresh.append(score)
             peak = jnp.maximum(peak, score)
@@ -418,7 +495,7 @@
         for m in range(news):
             weight = jnp.where(token >= m, jnp.exp(fresh[m] - peak), 0.0)
             total = total + weight
-            summed = summed + weight * fresh_ref[r, news + m : news + m + 1, :]
+            summed = summed + weight * fresh_values[m][r : r + 1]
         head[r] = summed / total
     for r in range(2):
         for a in range(size):
@@ -438,20 +515,21 @@
             device_id_type=MESH,
         )
 
-    for dt in list(range(1, tps)) + [0]:
+    for dt in (6, 5, 7, 4, 2, 1, 3, 0):
         to = (tp + dt) % tps
         part = jnp.dot(
             left,
             w_buf[:, pl.ds(pl.multiple_of(to * cols, cols), cols)],
             preferred_element_type=jnp.float32,
         )
-        s_out[dt] = part
         if dt:
+            s_out[dt] = jnp.concatenate([part[:, :wide], part[:, wide:]], axis=0).astype(jnp.bfloat16)
             s_copy(dt).start()
-    mixed = s_out[0]
-    for dt in range(1, tps):
+    mixed = part
+    for dt in (1, 3, 2, 4, 5, 7, 6):
         s_copy(dt).wait_recv()
-        mixed = mixed + s_in[dt]
+        folded = s_in[dt].astype(jnp.float32)
+        mixed = mixed + jnp.concatenate([folded[:8], folded[8:]], axis=1)
     mix_ref[...] = mixed.astype(jnp.bfloat16)
 
     q_done = [p_copy]
@@ -460,34 +538,14 @@
     for dt in range(1, tps):
         s_copy(dt).wait_send()
 
-    def x_drain(g, carry):
-        for dx in range(1, SIDE):
-            x_copy(g, dx).wait_send()
-            y_copy(g, dx).wait_send()
-        return carry
-
-    lax.fori_loop(0, groups, x_drain, 0)
-
-    def z_drain(k, carry):
-        @pl.when(z < SIDE - 1)
-        def _():
-            up_copy(k).wait_send()
-
-        @pl.when(z > 0)
-        def _():
-            down_copy(k).wait_send()
-
-        return carry
-
-    lax.fori_loop(0, units, z_drain, 0)
-
-
-def main_call(cap, collective_id, table, asking, fresh, keys, values, weight):
+
+def main_call(cap, collective_id, table, asking, fresh_key, fresh_value, keys, values, weight):
     slots, ctx, dim = keys.shape
     rows = ctx // (GROUPS * SIDE)
     tps = lax.axis_size("tp")
     cols = weight.shape[1] // tps
-    queries = asking.shape[1]
+    news, own, width = asking.shape
+    queries = news * (width // dim)
     unit = (2, rows, dim)
     units = GROUPS * cap
     bf16, f32 = jnp.bfloat16, jnp.float32
@@ -500,20 +558,25 @@
         out_shape=(
             jax.ShapeDtypeStruct(keys.shape, bf16),
             jax.ShapeDtypeStruct(values.shape, bf16),
-            jax.ShapeDtypeStruct((asking.shape[0] * fresh.shape[1] // 2, cols), bf16),
+            jax.ShapeDtypeStruct((news * own, cols), bf16),
         ),
         in_specs=[
             pl.BlockSpec(memory_space=pltpu.SMEM),
             vmem,
             vmem,
             vmem,
-            vmem,
+            pl.BlockSpec(memory_space=pl.ANY),
+            pl.BlockSpec(memory_space=pl.ANY),
             pl.BlockSpec(memory_space=pl.ANY),
         ],
         out_specs=(vmem, vmem, vmem),
         scratch_shapes=[
             pltpu.VMEM(weight.shape, bf16),
-            pltpu.VMEM(asking.shape, bf16),
+            pltpu.VMEM((slots + MOST, ctx, dim), bf16),
+            pltpu.VMEM((slots + MOST, ctx, dim), bf16),
+            pltpu.VMEM((own, queries, dim), f32),
+            pltpu.VMEM((own, queries, dim), bf16),
+            pltpu.VMEM((own, queries, dim), bf16),
             spread,
             spread,
             pltpu.VMEM((GROUPS, ITEMS + 2 * cap) + unit, bf16),
@@ -530,9 +593,10 @@
             pltpu.VMEM((2, 2, queries, dim), f32),
             pltpu.VMEM((2, queries, dim), f32),
             pltpu.VMEM((8, weight.shape[0]), f32),
-            pltpu.VMEM((tps, 8, cols), f32),
-            pltpu.VMEM((tps, 8, cols), f32),
+            pltpu.VMEM((tps, 16, cols // 2), bf16),
+            pltpu.VMEM((tps, 16, cols // 2), bf16),
             dma,
+            dma((2,)),
             dma((2,)),
             dma((GROUPS, SIDE - 1)),
             dma((GROUPS, SIDE - 1)),
@@ -550,7 +614,7 @@
             collective_id=collective_id, has_side_effects=True, vmem_limit_bytes=56 << 20
         ),
         name=f"move_attend_{cap}",
-    )(table, asking, fresh, keys, values, weight)
+    )(table, asking, fresh_key, fresh_value, keys, values, weight)
 
 
 def on_device(
@@ -567,7 +631,6 @@
 ):
     _, slots, ctx, _, dim = keys_cache.shape
     news, own = queries.shape[:2]
-    size = queries.shape[2] // dim
     smem = pl.BlockSpec(memory_space=pltpu.SMEM)
     table = pl.pallas_call(
         plan_kernel,
@@ -577,13 +640,9 @@
         scratch_shapes=[pltpu.SMEM((16,), jnp.int32), pltpu.SMEM((16,), jnp.int32)],
         name="plan",
     )(partner, chosen.T, lengths.T, dest_slot.T)
-    asking = queries.reshape(news, own, size, dim).transpose(1, 0, 2, 3)
-    asking = asking.reshape(own, news * size, dim)
-    fresh = jnp.concatenate([fresh_keys, fresh_values], axis=0).transpose(1, 0, 2)
-    fresh = fresh.astype(jnp.float32)
     keys = keys_cache.reshape(slots, ctx, dim)
     values = values_cache.reshape(slots, ctx, dim)
-    args = (table, asking, fresh, keys, values, out_weight)
+    args = (table, queries, fresh_keys, fresh_values, keys, values, out_weight)
     if len(CAPS) == 1:
         moved_keys, moved_values, mixed = main_call(CAPS[0], 0, *args)
     else:

time: 75.4 us -> 66.8 us (0.89)
  Pallas kernels: 68.3 us -> 61.9 us
  local copies, waits for them, and re-layouts: 5.24 us -> 3.13 us
    pallas_call x1, Pallas kernels: 66.4 us -> 60 us  [main_call(): pl.pallas_call(functools.partial(main_kernel, cap), out_shape=(jax.ShapeD...]
    unnamed x4 -> x2, local copies, waits for them, and re-layouts: 3.31 us -> 1.94 us
where the time goes in v3:
time: 66.8 us; the launch traced here: 66.6 us
  Pallas kernels  61.9 us (93%)
  local copies, waits for them, and re-layouts  3.13 us (5%)
  between operations  1.3 us (2%)
    pallas_call x1, Pallas kernels, main_call(): pl.pallas_call(functools.partial(main_kernel, cap), out_shape=(jax.ShapeD...  60 us
    unnamed x2, local copies, waits for them, and re-layouts  1.94 us
    pallas_call x1, Pallas kernels, on_device(): pl.pallas_call(plan_kernel, out_shape=jax.ShapeDtypeStruct((TABLE,), jnp....  1.89 us

profile of v3, /device:TPU:1, one launch (start us, length us, event | category | flops | bytes accessed | tf_op | source)
XLA Modules:
  0.0 66.6 jit_solution(17230890684392557556)
XLA Ops:
  0.6 1.9 %plan.1 = s32[64]{0:T(128)S(1)} custom-call(s32[16]{0:T(128)} %partner.1, s32[4,16]{1,0:T(4,128)} %bitcast.22, s32[4,16]{1,0:T(4,128)} %bitcast.23, s32[4,16]{1,0:T(4,128)} %bitcast.24), custom_call_target="tpu_custom_call" | custom-call | tf_op jit(solution)/shard_map/plan/pallas_call | solution.py:635
  2.5 0.6 slice.3
  3.8 60.3 %conditional.1 = ((bf16[4,1024,128]{2,1,0:T(8,128)(2,1)S(1)}, bf16[4,1024,128]{2,1,0:T(8,128)(2,1)S(1)}, bf16[8,512]{1,0:T(8,128)(2,1)S(1)})) conditional(s32[]{:T(128)} %bitcast.3, (s32[64]{0:T(128)S(1)}, bf16[4,2,1024]{2,1,0:T(2,128)(2,1)}, bf16[4,2,128]{2,1,0:T(2,128)(2,1)}, bf16[4,2,128]{2,1,0:T(2,128)(2,1)}, ...), branch_computations={%region_0.0_spmd, %region_1.0_spmd, %region_2.0_spmd, %region_3.0_... | conditional | bytes 8 | solution.py:649
  3.8 60.0 %move_attend_6.1 = (bf16[4,1024,128]{2,1,0:T(8,128)(2,1)S(1)}, bf16[4,1024,128]{2,1,0:T(8,128)(2,1)S(1)}, bf16[8,512]{1,0:T(8,128)(2,1)S(1)}) custom-call(s32[64]{0:T(128)S(1)} %get-tuple-element.115.table, bf16[4,2,1024]{2,1,0:T(2,128)(2,1)} %get-tuple-element.116.raw_ref, bf16[4,2,128]{2,1,0:T(2,128)(2,1)} %get-tuple-element.117.fk_ref, ...), custom_call_target="tpu_custom_call" | custom-call | tf_op jit(solution)/shard_map/cond/branch_1_fun/move_attend_6/pallas_call | solution.py:556
  64.0 0.6 reshape.74
  64.6 1.0 %copy.33 = bf16[1,4,1024,1,128]{4,2,3,1,0:T(8,128)(2,1)} copy(bf16[1,4,1024,1,128]{4,2,3,1,0:T(8,128)(2,1)S(1)} %bitcast.20) | data formatting | bytes 2097152
  65.6 1.0 %copy.34 = bf16[1,4,1024,1,128]{4,2,3,1,0:T(8,128)(2,1)} copy(bf16[1,4,1024,1,128]{4,2,3,1,0:T(8,128)(2,1)S(1)} %bitcast.21) | data formatting | bytes 2097152

commit v4 on v3

v4 whole, which is shorter than its diff:
```python
import functools

import jax
import jax.numpy as jnp
from jax import lax
from jax.experimental import pallas as pl
from jax.experimental.pallas import tpu as pltpu
from jax.sharding import PartitionSpec as P

MESH = pl.DeviceIdType.MESH
LOW = -1e30
SLOTS = 4
MOST = 2
SIDE = 4
ITEMS = SIDE * MOST
WIDEST = ITEMS * 2
CAPS = (5, 6, 7, 8, 9, 10, 16)
GROUPS = 4
SKEW = 6
ATTEND = 2
FIRST = 1
LATER = 12
PAIR = 8
ASKING = 5
FAR, NEAR = (6, 5, 7, 4), (2, 1, 3)
UP, DOWN, OUT, SEL, SPAN, PICK, NONE, ASK, ASKED, TABLE = 0, 16, 32, 40, 44, 48, 50, 52, 54, 56


def where_am_i():
    inst = lax.axis_index("inst")
    chip = inst // 2
    return inst % 2, chip, chip // SIDE, chip % SIDE


def plan_kernel(partner, chosen, lengths, dest, table, variant, count, start):
    _, me, _, z = where_am_i()
    sent = []
    for i in range(16):
        count[i] = 0
    for s in range(16):
        sent.append(sum(chosen[r, s] for r in range(SLOTS)))
        cls = (s % SIDE) * SIDE + partner[s] % SIDE
        count[cls] = count[cls] + sent[s]
    n = [[count[a * SIDE + b] for b in range(SIDE)] for a in range(SIDE)]

    def flip(a, b, down):
        return n[3 - a][3 - b] if down else n[a][b]

    need = 0
    for down in (False, True):
        f = functools.partial(flip, down=down)
        need = functools.reduce(
            jnp.maximum,
            (
                need,
                f(0, 1) + f(0, 2) + f(0, 3),
                f(0, 2) + f(0, 3) + f(1, 2) + f(1, 3),
                f(0, 3) + f(1, 3) + f(2, 3),
            ),
        )
    which, cap = 0, CAPS[0]
    for i in range(1, len(CAPS)):
        which = jnp.where(need > CAPS[i - 1], i, which)
        cap = jnp.where(need > CAPS[i - 1], CAPS[i], cap)
    variant[0] = which
    for down in (False, True):
        f = functools.partial(flip, down=down)
        places = {
            (0, 3): 0,
            (1, 3): f(0, 3),
            (1, 2): f(0, 3) + f(1, 3),
            (0, 2): cap - f(0, 2),
            (0, 1): f(0, 3),
            (2, 3): f(0, 3) + f(1, 3),
        }
        for (a, b), place in places.items():
            start[(3 - a) * SIDE + 3 - b if down else a * SIDE + b] = place
    for a in range(SIDE):
        start[a * SIDE + a] = 0
    for c in range(WIDEST):
        table[UP + c] = jnp.where(z == 0, 0, ITEMS + c)
        table[DOWN + c] = jnp.where(z == SIDE - 1, 0, ITEMS + cap + c)
    for i in range(OUT, TABLE):
        table[i] = 0
    source = 0
    for s in range(16):
        d = partner[s]
        source = jnp.where(d == me, s, source)
        zs, xs = s % SIDE, s // SIDE
        zd, xd = d % SIDE, d // SIDE
        base = start[zs * SIDE + zd]
        start[zs * SIDE + zd] = base + sent[s]
        for j in range(MOST):
            valid = j < sent[s]
            leaves = valid & (zs == z) & (zd != zs)
            place = jnp.where(zd > zs, UP, DOWN) + base + j
            table[jnp.where(leaves, place, NONE)] = xs * MOST + j
            lands = valid & (zd == z)
            kept = jnp.where(zs < z, ITEMS + base + j, ITEMS + cap + base + j)
            kept = jnp.where(zs == z, xs * MOST + j, kept)
            table[jnp.where(lands, OUT + xd * MOST + j, NONE)] = kept
    mine, theirs = 0, 0
    for r in range(SLOTS):
        table[SEL + r] = r
        table[SPAN + r] = lengths[r, me]
    for r in range(SLOTS):
        go = chosen[r, me] == 1
        table[jnp.where(go, PICK + mine, NONE)] = r
        table[jnp.where(go, ASK + mine, NONE)] = partner[me] * 2 + dest[r, me] % 2
        table[jnp.where(go, ASKED + mine, NONE)] = dest[r, me] // 2
        mine = mine + jnp.where(go, 1, 0)
        come = chosen[r, source] == 1
        slot = dest[r, source]
        theirs = theirs + jnp.where(come, 1, 0)
        table[jnp.where(come, SEL + slot, NONE)] = SLOTS - 1 + theirs


def main_kernel(cap, table, *refs):
    (raw_ref, fk_ref, fv_ref, k_hbm, v_hbm, w_hbm, mk_ref, mv_ref, mix_ref, *refs) = refs
    (w_buf, k_ref, v_ref, q_rows, q_ref, q_peer, *refs) = refs
    (z_in, line_q, x_in_q, all_q, pick_q, peer_q, slot_q, part, gone, *refs) = refs
    (x_out, x_in, pool, up_out, up_in, down_out, down_in, y_out, y_in, *refs) = refs
    (px_out, px_in, p_pool, p_up_out, p_up_in, p_down_out, p_down_in, py_out, py_in, *refs) = refs
    (p_out, p_in, head, lhs, s_out, s_in, *refs) = refs
    (w_sem, kv_sem, q_sem, zq_sem, xq_sem, cq_sem, p_sem, s_sem, *refs) = refs
    (x_sem, up_sem, down_sem, y_sem, px_sem, p_up_sem, p_down_sem, py_sem) = refs
    groups = x_out.shape[0]
    rows = x_out.shape[4]
    thin = px_out.shape[3]
    ctx = k_ref.shape[1]
    span = ctx // groups
    tps = s_out.shape[0]
    cols = mix_ref.shape[1]
    wide = cols // 2
    news, _, width = raw_ref.shape
    dim = k_ref.shape[2]
    size = width // dim
    queries = news * size
    blocks = groups + 1
    special = groups // 2
    units = blocks * cap
    scaling = dim**-0.5
    half, chip, x, z = where_am_i()
    inst = lax.axis_index("inst")
    tp = lax.axis_index("tp")
    peer = (inst + 1 - 2 * half, tp)

    def along_x(dx):
        return (((x + dx) % SIDE * SIDE + z) * 2 + half, tp)

    def along_z(dz):
        return ((x * SIDE + (z + dz) % SIDE) * 2 + half, tp)

    above = (inst + 2, tp)
    below = (inst - 2, tp)

    def remote(source, target, sems, device):
        return pltpu.make_async_remote_copy(
            source, target, sems[0], sems[1], device_id=device, device_id_type=MESH
        )

    k_copy = pltpu.make_async_copy(k_hbm, k_ref.at[:SLOTS], kv_sem.at[0])
    v_copy = pltpu.make_async_copy(v_hbm, v_ref.at[:SLOTS], kv_sem.at[1])
    k_copy.start()
    v_copy.start()
    barrier = pltpu.get_barrier_semaphore()

    def greet(device):
        pl.semaphore_signal(barrier, inc=1, device_id=device, device_id_type=MESH)

    greet(peer)
    for d in range(1, SIDE):
        greet(along_x(d))
        greet(along_z(d))
    for dt in range(1, tps):
        greet((inst, (tp + dt) % tps))
    w_copy = pltpu.make_async_copy(w_hbm, w_buf, w_sem)

    for n in range(news):
        raw = raw_ref[n].astype(jnp.float32)
        for r in range(2):
            for a in range(size):
                q_rows[r, n * size + a : n * size + a + 1, :] = raw[
                    r : r + 1, a * dim : (a + 1) * dim
                ]
    for r in range(2):
        q_ref[r] = q_rows[r].astype(jnp.bfloat16)
    k_copy.wait()
    v_copy.wait()

    def stage(g):
        for dx in range(SIDE):
            to = (x + dx) % SIDE
            at = pl.ds(pl.multiple_of((g * SIDE + to) * rows, rows), rows)
            for j in range(MOST):
                slot = table[PICK + j]
                for kv, ref in enumerate((k_ref, v_ref)):
                    piece = ref[slot, at, :]
                    if dx == 0:
                        pool[g, x * MOST + j, kv] = piece
                    else:
                        x_out[g, dx - 1, j, kv] = piece

    def x_copy(g, dx):
        i = dx - 1
        sems = (x_sem.at[0, g, i], x_sem.at[1, g, i])
        return remote(x_out.at[g, i], x_in.at[g, i], sems, along_x(dx))

    def y_copy(g, dx):
        i = dx - 1
        sems = (y_sem.at[0, g, i], y_sem.at[1, g, i])
        return remote(y_out.at[g, i], y_in.at[g, i], sems, along_x(dx))

    def px_copy(dx):
        i = dx - 1
        return remote(
            px_out.at[i], px_in.at[i], (px_sem.at[0, i], px_sem.at[1, i]), along_x(dx)
        )

    def py_copy(dx):
        i = dx - 1
        return remote(
            py_out.at[i], py_in.at[i], (py_sem.at[0, i], py_sem.at[1, i]), along_x(dx)
        )

    def up_copy(k):
        return remote(up_out.at[k], up_in.at[k], (up_sem.at[0, k], up_sem.at[1, k]), above)

    def down_copy(k):
        return remote(
            down_out.at[k], down_in.at[k], (down_sem.at[0, k], down_sem.at[1, k]), below
        )

    def p_up_copy(c):
        sems = (p_up_sem.at[0, c], p_up_sem.at[1, c])
        return remote(p_up_out.at[c], p_up_in.at[c], sems, above)

    def p_down_copy(c):
        sems = (p_down_sem.at[0, c], p_down_sem.at[1, c])
        return remote(p_down_out.at[c], p_down_in.at[c], sems, below)

    def zq_copy(dz):
        i = dz - 1
        return remote(q_ref, z_in.at[i], (zq_sem.at[0, i], zq_sem.at[1, i]), along_z(dz))

    def xq_copy(dx):
        i = dx - 1
        return remote(line_q, x_in_q.at[i], (xq_sem.at[0, i], xq_sem.at[1, i]), along_x(dx))

    q_copy = remote(q_ref, q_peer, (q_sem.at[0], q_sem.at[1]), peer)
    cq_copy = remote(pick_q, peer_q, (cq_sem.at[0], cq_sem.at[1]), peer)
    p_copy = remote(p_out, p_in, (p_sem.at[0], p_sem.at[1]), peer)

    def s_copy(dt):
        sems = (s_sem.at[0, dt], s_sem.at[1, dt])
        return remote(s_out.at[dt], s_in.at[dt], sems, (inst, (tp + dt) % tps))

    def x_start(g):
        for dx in (1, 3, 2):
            x_copy(g, dx).start()

    stage(0)
    pl.semaphore_wait(barrier, 1 + 2 * (SIDE - 1) + tps - 1)
    x_start(0)
    for dz in range(1, SIDE):
        zq_copy(dz).start()
    q_copy.start()

    def stage_rest(g, carry):
        stage(g)
        return carry

    lax.fori_loop(1, groups, stage_rest, 0)

    nearest = jnp.minimum(z, SIDE - 1 - z) * SKEW
    farthest = jnp.maximum(z, SIDE - 1 - z) * SKEW + cap - 1

    factor = -(-(1 << 16) // cap)

    def split(k):
        b = lax.shift_right_arithmetic(k * factor, 16)
        return b, k - b * cap

    def group_of(b):
        return jnp.where(b > special, b - 1, b)

    def spread_queries():
        line_q[z] = q_ref[...]
        for dz in range(1, SIDE):
            zq_copy(dz).wait_recv()
            line_q[(z + SIDE - dz) % SIDE] = z_in[dz - 1]
        for dx in (1, 3, 2):
            xq_copy(dx).start()
        for i in range(SIDE):
            for r in range(2):
                all_q[(x * SIDE + i) * 2 + r] = line_q[i, r]

    def pick_queries():
        for dx in range(1, SIDE):
            xq_copy(dx).wait_recv()
            origin = (x + SIDE - dx) % SIDE
            for i in range(SIDE):
                for r in range(2):
                    all_q[(origin * SIDE + i) * 2 + r] = x_in_q[dx - 1, i, r]
        for j in range(MOST):
            pick_q[j] = all_q[table[ASK + j]]
        cq_copy.start()

    def own_queries():
        q_copy.wait_recv()
        for r in range(2):
            slot_q[half * 2 + r] = q_ref[r]
            slot_q[(1 - half) * 2 + r] = q_peer[r]

    def far_queries():
        cq_copy.wait_recv()
        for j in range(MOST):
            here = table[ASKED + j] == half
            slot_q[SLOTS + j] = jnp.where(here, pick_q[j], peer_q[j])

    lane = lax.broadcasted_iota(jnp.int32, (queries, dim), 1)

    def attend(asking, slot, out):
        scores = (
            lax.dot_general(
                asking,
                k_ref[slot],
                (((1,), (1,)), ((), ())),
                preferred_element_type=jnp.float32,
            )
            * scaling
        )
        spot = half * ctx + lax.broadcasted_iota(jnp.int32, (queries, ctx), 1)
        usable = spot < table[SPAN + slot]
        highest = jnp.max(jnp.where(usable, scores, LOW), axis=1, keepdims=True)
        weights = jnp.where(usable, jnp.exp(scores - highest), 0.0)
        total = jnp.sum(weights, axis=1, keepdims=True)
        out[0] = jnp.dot(
            weights.astype(jnp.bfloat16), v_ref[slot], preferred_element_type=jnp.float32
        )
        out[1] = jnp.where(lane < 64, highest, total)

    def px_start():
        for dx in range(SIDE):
            to = (x + dx) % SIDE
            at = pl.ds(pl.multiple_of(to * thin, thin), thin)
            for j in range(MOST):
                for kv in range(2):
                    piece = gone[j, kv, at, :]
                    if dx == 0:
                        p_pool[x * MOST + j, kv] = piece
                    else:
                        px_out[dx - 1, j, kv] = piece
        for dx in (1, 3, 2):
            px_copy(dx).start()

    def x_arrive(g):
        for dx in range(1, SIDE):
            x_copy(g, dx).wait_recv()
            origin = (x + SIDE - dx) % SIDE
            for j in range(MOST):
                pool[g, origin * MOST + j] = x_in[g, dx - 1, j]

    def px_arrive():
        for dx in range(1, SIDE):
            px_copy(dx).wait_recv()
            origin = (x + SIDE - dx) % SIDE
            for j in range(MOST):
                p_pool[origin * MOST + j] = px_in[dx - 1, j]

    def y_start(g):
        for dx in (1, 3, 2):
            to = (x + dx) % SIDE
            for j in range(MOST):
                y_out[g, dx - 1, j] = pool[g, table[OUT + to * MOST + j]]
            y_copy(g, dx).start()

    def py_start():
        for dx in (1, 3, 2):
            to = (x + dx) % SIDE
            for j in range(MOST):
                py_out[dx - 1, j] = p_pool[table[OUT + to * MOST + j]]
            py_copy(dx).start()

    def settle(g):
        for dx in range(SIDE):
            origin = (x + SIDE - dx) % SIDE
            at = pl.ds(pl.multiple_of((g * SIDE + origin) * rows, rows), rows)
            if dx:
                y_copy(g, dx).wait_recv()
            for j in range(MOST):
                if dx:
                    piece = y_in[g, dx - 1, j]
                else:
                    piece = pool[g, table[OUT + x * MOST + j]]
                k_ref[SLOTS + j, at, :] = piece[0]
                v_ref[SLOTS + j, at, :] = piece[1]

    def emit(g):
        at = pl.ds(pl.multiple_of(g * span, span), span)
        for slot in range(SLOTS):
            source = table[SEL + slot]
            mk_ref[slot, at, :] = k_ref[source, at, :]
            mv_ref[slot, at, :] = v_ref[source, at, :]

    def p_settle():
        for dx in range(SIDE):
            origin = (x + SIDE - dx) % SIDE
            at = pl.ds(pl.multiple_of(origin * thin, thin), thin)
            if dx:
                py_copy(dx).wait_recv()
            for j in range(MOST):
                if dx:
                    piece = py_in[dx - 1, j]
                else:
                    piece = p_pool[table[OUT + x * MOST + j]]
                part[SLOTS + j, 0, at, :] = piece[0]
                part[SLOTS + j, 1, at, :] = piece[1]
        for r in range(2):
            p_out[r] = part[table[SEL + (1 - half) * 2 + r]]
        p_copy.start()

    def combine():
        p_copy.wait_recv()
        token = lax.broadcasted_iota(jnp.int32, (queries, 1), 0) // size
        fresh_keys = [fk_ref[m].astype(jnp.float32) for m in range(news)]
        fresh_values = [fv_ref[m].astype(jnp.float32) for m in range(news)]
        for r in range(2):
            mine = part[table[SEL + half * 2 + r]]
            top_a, tot_a = mine[1][:, :1], mine[1][:, 64:65]
            top_b, tot_b = p_in[r, 1][:, :1], p_in[r, 1][:, 64:65]
            asking = q_rows[r]
            peak = jnp.maximum(top_a, top_b)
            fresh = []
            for m in range(news):
                score = jnp.sum(asking * fresh_keys[m][r : r + 1], axis=1, keepdims=True)
                score = jnp.where(token >= m, score * scaling, LOW)
                fresh.append(score)
                peak = jnp.maximum(peak, score)
            scale_a = jnp.exp(top_a - peak)
            scale_b = jnp.exp(top_b - peak)
            summed = mine[0] * scale_a + p_in[r, 0] * scale_b
            total = tot_a * scale_a + tot_b * scale_b
            for m in range(news):
                weight = jnp.where(token >= m, jnp.exp(fresh[m] - peak), 0.0)
                total = total + weight
                summed = summed + weight * fresh_values[m][r : r + 1]
            head[r] = summed / total
        for r in range(2):
            for a in range(size):
                for n in range(news):
                    lhs[n * 2 + r : n * 2 + r + 1, a * dim : (a + 1) * dim] = head[
                        r, n * size + a : n * size + a + 1, :
                    ]
        w_copy.wait()

    def project(dt):
        to = (tp + dt) % tps
        part_out = jnp.dot(
            lhs[...].astype(jnp.bfloat16),
            w_buf[:, pl.ds(pl.multiple_of(to * cols, cols), cols)],
            preferred_element_type=jnp.float32,
        )
        if dt == 0:
            return part_out
        folded = jnp.concatenate([part_out[:, :wide], part_out[:, wide:]], axis=0)
        s_out[dt] = folded.astype(jnp.bfloat16)
        s_copy(dt).start()

    spread_queries()
    for g in range(1, 1 + FIRST):
        x_start(g)
    w_copy.start()

    settled = [(g, (g if g < special else g + 1) * cap + LATER) for g in range(groups - 1)]

    pair_at = min(special * cap + PAIR, groups * cap - 2)

    def step(t, carry):
        early = t - nearest

        @pl.when((early >= 0) & (early < units))
        def _():
            b, c = split(early)

            @pl.when((c == 0) & (b != special))
            def _():
                x_arrive(group_of(b))

            @pl.when(early == special * cap)
            def _():
                px_arrive()

            for g in range(1 + FIRST, groups):

                @pl.when(early == 5 + (g - 1 - FIRST) * cap)
                def _():
                    x_start(g)

            @pl.when(early == ASKING)
            def _():
                pick_queries()

            @pl.when(early == ASKING + 2)
            def _():
                far_queries()

            for j in range(MOST):

                @pl.when(early == ASKING + 2 + j)
                def _():
                    attend(slot_q[SLOTS + j], table[PICK + j], gone.at[j])

            @pl.when(early == ASKING + 2 + MOST)
            def _():
                px_start()

            @pl.when(early == ASKING + 3 + MOST)
            def _():
                own_queries()

            for slot in range(SLOTS):

                @pl.when(early == ASKING + 3 + MOST + slot * ATTEND)
                def _():
                    attend(slot_q[slot], slot, part.at[slot])

        k = t - z * SKEW

        @pl.when((k >= 0) & (k < units))
        def _():
            b, c = split(k)

            @pl.when(b != special)
            def _():
                g = group_of(b)
                i = g * cap + c

                @pl.when(z > 0)
                def _():
                    up_copy(i).wait_recv()
                    pool[g, ITEMS + c] = up_in[i]

                @pl.when(z < SIDE - 1)
                def _():
                    up_out[i] = pool[g, table[UP + c]]
                    up_copy(i).start()

            @pl.when(b == special)
            def _():
                @pl.when(z > 0)
                def _():
                    p_up_copy(c).wait_recv()
                    p_pool[ITEMS + c] = p_up_in[c]

                @pl.when(z < SIDE - 1)
                def _():
                    p_up_out[c] = p_pool[table[UP + c]]
                    p_up_copy(c).start()

        m = t - (SIDE - 1 - z) * SKEW

        @pl.when((m >= 0) & (m < units))
        def _():
            b, c = split(m)

            @pl.when(b != special)
            def _():
                g = group_of(b)
                i = g * cap + c

                @pl.when(z < SIDE - 1)
                def _():
                    down_copy(i).wait_recv()
                    pool[g, ITEMS + cap + c] = down_in[i]

                @pl.when(z > 0)
                def _():
                    down_out[i] = pool[g, table[DOWN + c]]
                    down_copy(i).start()

            @pl.when(b == special)
            def _():
                @pl.when(z < SIDE - 1)
                def _():
                    p_down_copy(c).wait_recv()
                    p_pool[ITEMS + cap + c] = p_down_in[c]

                @pl.when(z > 0)
                def _():
                    p_down_out[c] = p_pool[table[DOWN + c]]
                    p_down_copy(c).start()

        late = t - farthest

        @pl.when(late >= 0)
        def _():
            b, c = split(late)

            @pl.when((c == 0) & (b != special) & (b < blocks))
            def _():
                y_start(group_of(b))

            @pl.when(late == special * cap)
            def _():
                py_start()

            @pl.when(late == pair_at)
            def _():
                p_settle()

            @pl.when(late == pair_at + 2)
            def _():
                combine()

            for g, at in settled:
                if at <= groups * cap:

                    @pl.when(late == at)
                    def _():
                        settle(g)

                    @pl.when(late == at)
                    def _():
                        emit(g)

        return carry

    lax.fori_loop(0, units + (SIDE - 1) * SKEW, step, 0)

    for dt in FAR + NEAR:
        project(dt)
    mixed = project(0)
    for g, at in settled:
        if at > groups * cap:
            settle(g)
            emit(g)
    settle(groups - 1)
    emit(groups - 1)

    def x_drain(g, carry):
        for dx in range(1, SIDE):
            x_copy(g, dx).wait_send()
            y_copy(g, dx).wait_send()
        return carry

    lax.fori_loop(0, groups, x_drain, 0)
    for d in range(1, SIDE):
        px_copy(d).wait_send()
        py_copy(d).wait_send()
        zq_copy(d).wait_send()
        xq_copy(d).wait_send()
    q_copy.wait_send()
    cq_copy.wait_send()
    p_copy.wait_send()

    @pl.when(z < SIDE - 1)
    def _():
        def drain(k, carry):
            up_copy(k).wait_send()
            return carry

        def p_drain(k, carry):
            p_up_copy(k).wait_send()
            return carry

        lax.fori_loop(0, groups * cap, drain, 0)
        lax.fori_loop(0, cap, p_drain, 0)

    @pl.when(z > 0)
    def _():
        def drain(k, carry):
            down_copy(k).wait_send()
            return carry

        def p_drain(k, carry):
            p_down_copy(k).wait_send()
            return carry

        lax.fori_loop(0, groups * cap, drain, 0)
        lax.fori_loop(0, cap, p_drain, 0)

    for dt in NEAR + FAR:
        s_copy(dt).wait_recv()
        folded = s_in[dt].astype(jnp.float32)
        mixed = mixed + jnp.concatenate([folded[:8], folded[8:]], axis=1)
        s_copy(dt).wait_send()
    mix_ref[...] = mixed.astype(jnp.bfloat16)


def main_call(cap, collective_id, table, asking, fresh_key, fresh_value, keys, values, weight):
    slots, ctx, dim = keys.shape
    rows = ctx // (GROUPS * SIDE)
    tps = lax.axis_size("tp")
    cols = weight.shape[1] // tps
    news, own, width = asking.shape
    queries = news * (width // dim)
    unit = (2, rows, dim)
    thin = (2, queries // SIDE, dim)
    bf16, f32 = jnp.bfloat16, jnp.float32
    vmem = pl.BlockSpec(memory_space=pltpu.VMEM)
    hbm = pl.BlockSpec(memory_space=pl.ANY)
    dma = pltpu.SemaphoreType.DMA
    cache = pltpu.VMEM((slots + MOST, ctx, dim), bf16)
    asked = pltpu.VMEM((own, queries, dim), bf16)
    spread = pltpu.VMEM((GROUPS, SIDE - 1, MOST) + unit, bf16)
    line = pltpu.VMEM((GROUPS * cap,) + unit, bf16)
    thin_spread = pltpu.VMEM((SIDE - 1, MOST) + thin, f32)
    thin_line = pltpu.VMEM((cap,) + thin, f32)
    pair = pltpu.VMEM((2, 2, queries, dim), f32)
    sums = pltpu.VMEM((tps, 2 * news * own, cols // 2), bf16)
    return pl.pallas_call(
        functools.partial(main_kernel, cap),
        out_shape=(
            jax.ShapeDtypeStruct(keys.shape, bf16),
            jax.ShapeDtypeStruct(values.shape, bf16),
            jax.ShapeDtypeStruct((news * own, cols), bf16),
        ),
        in_specs=[pl.BlockSpec(memory_space=pltpu.SMEM), vmem, vmem, vmem, hbm, hbm, hbm],
        out_specs=(vmem, vmem, vmem),
        scratch_shapes=[
            pltpu.VMEM(weight.shape, bf16),
            cache,
            cache,
            pltpu.VMEM((own, queries, dim), f32),
            asked,
            asked,
            pltpu.VMEM((SIDE - 1, own, queries, dim), bf16),
            pltpu.VMEM((SIDE, own, queries, dim), bf16),
            pltpu.VMEM((SIDE - 1, SIDE, own, queries, dim), bf16),
            pltpu.VMEM((SIDE * SIDE * own, queries, dim), bf16),
            asked,
            asked,
            pltpu.VMEM((slots + MOST, queries, dim), bf16),
            pltpu.VMEM((slots + MOST, 2, queries, dim), f32),
            pair,
            spread,
            spread,
            pltpu.VMEM((GROUPS, ITEMS + 2 * cap) + unit, bf16),
            line,
            line,
            line,
            line,
            spread,
            spread,
            thin_spread,
            thin_spread,
            pltpu.VMEM((ITEMS + 2 * cap,) + thin, f32),
            thin_line,
            thin_line,
            thin_line,
            thin_line,
            thin_spread,
            thin_spread,
            pair,
            pair,
            pltpu.VMEM((own, queries, dim), f32),
            pltpu.VMEM((news * own, weight.shape[0]), f32),
            sums,
            sums,
            dma,
            dma((2,)),
            dma((2,)),
            dma((2, SIDE - 1)),
            dma((2, SIDE - 1)),
            dma((2,)),
            dma((2,)),
            dma((2, tps)),
            dma((2, GROUPS, SIDE - 1)),
            dma((2, GROUPS * cap)),
            dma((2, GROUPS * cap)),
            dma((2, GROUPS, SIDE - 1)),
            dma((2, SIDE - 1)),
            dma((2, cap)),
            dma((2, cap)),
            dma((2, SIDE - 1)),
        ],
        compiler_params=pltpu.CompilerParams(
            collective_id=collective_id, has_side_effects=True, vmem_limit_bytes=56 << 20
        ),
        name=f"move_attend_{cap}",
    )(table, asking, fresh_key, fresh_value, keys, values, weight)


def on_device(
    keys_cache,
    values_cache,
    queries,
    fresh_keys,
    fresh_values,
    out_weight,
    partner,
    chosen,
    lengths,
    dest_slot,
):
    _, slots, ctx, _, dim = keys_cache.shape
    news, own = queries.shape[:2]
    smem = pl.BlockSpec(memory_space=pltpu.SMEM)
    table, variant = pl.pallas_call(
        plan_kernel,
        out_shape=(
            jax.ShapeDtypeStruct((TABLE,), jnp.int32),
            jax.ShapeDtypeStruct((1,), jnp.int32),
        ),
        in_specs=[smem] * 4,
        out_specs=(smem, smem),
        scratch_shapes=[pltpu.SMEM((16,), jnp.int32), pltpu.SMEM((16,), jnp.int32)],
        name="plan",
    )(partner, chosen.T, lengths.T, dest_slot.T)
    keys = keys_cache.reshape(slots, ctx, dim)
    values = values_cache.reshape(slots, ctx, dim)
    args = (table, queries, fresh_keys, fresh_values, keys, values, out_weight)
    if len(CAPS) == 1:
        moved_keys, moved_values, mixed = main_call(CAPS[0], 0, *args)
    else:
        moved_keys, moved_values, mixed = lax.switch(
            variant[0],
            [functools.partial(main_call, cap, i) for i, cap in enumerate(CAPS)],
            *args,
        )
    return (
        moved_keys.reshape(keys_cache.shape),
        moved_values.reshape(values_cache.shape),
        mixed.reshape(news, own, mixed.shape[1]),
    )


def solution(mesh):
    in_specs = (
        P("inst", None, None, "tp", None),
        P("inst", None, None, "tp", None),
        P(None, "inst", "tp"),
        P(None, "inst", "tp"),
        P(None, "inst", "tp"),
        P("tp", None),
        P(),
        P(),
        P(),
        P(),
    )
    out_specs = (
        P("inst", None, None, "tp", None),
        P("inst", None, None, "tp", None),
        P(None, "inst", "tp"),
    )
    return jax.shard_map(
        on_device, mesh=mesh, in_specs=in_specs, out_specs=out_specs, check_vma=False
    )
```

time: 66.8 us -> 63.8 us (0.955); the launches traced: 66.6 us -> 64.9 us
  Pallas kernels: 61.9 us -> 60.5 us
    pallas_call x1, Pallas kernels: 60 us -> 58.6 us  [main_call(): pl.pallas_call(functools.partial(main_kernel, cap), out_shape=(jax.ShapeD...]
where the time goes in v4:
time: 63.8 us; the launch traced here: 64.9 us
  Pallas kernels  60.5 us (95%)
  local copies, waits for them, and re-layouts  2.55 us (4%)
  between operations  1.3 us (2%)
    pallas_call x1, Pallas kernels, main_call(): pl.pallas_call(functools.partial(main_kernel, cap), out_shape=(jax.ShapeD...  58.6 us
    unnamed x2, local copies, waits for them, and re-layouts  1.94 us
    pallas_call x1, Pallas kernels, on_device(): pl.pallas_call(plan_kernel, out_shape=(jax.ShapeDtypeStruct((TABLE,), jnp...  1.92 us

profile of v4, /device:TPU:1, one launch (start us, length us, event | category | flops | bytes accessed | tf_op | source)
XLA Modules:
  0.0 64.9 jit_solution(15066917502429123686)
XLA Ops:
  0.6 1.9 %plan.1 = (s32[56]{0:T(128)S(1)}, s32[1]{0:T(128)}) custom-call(s32[16]{0:T(128)} %partner.1, s32[4,16]{1,0:T(4,128)} %bitcast.24, s32[4,16]{1,0:T(4,128)} %bitcast.25, s32[4,16]{1,0:T(4,128)} %bitcast.26), custom_call_target="tpu_custom_call" | custom-call | tf_op jit(solution)/shard_map/plan/pallas_call | solution.py:800
  3.2 59.1 %conditional.1 = ((bf16[4,1024,128]{2,1,0:T(8,128)(2,1)S(1)}, bf16[4,1024,128]{2,1,0:T(8,128)(2,1)S(1)}, bf16[8,512]{1,0:T(8,128)(2,1)S(1)})) conditional(s32[]{:T(128)} %bitcast.3, (s32[56]{0:T(128)S(1)}, bf16[4,2,1024]{2,1,0:T(2,128)(2,1)}, bf16[4,2,128]{2,1,0:T(2,128)(2,1)}, bf16[4,2,128]{2,1,0:T(2,128)(2,1)}, ...), branch_computations={%region_0.0_spmd, %region_1.0_spmd, %region_2.0_spmd, %region_3.0_... | conditional | bytes 8 | solution.py:817
  3.2 58.6 %move_attend_7.1 = (bf16[4,1024,128]{2,1,0:T(8,128)(2,1)S(1)}, bf16[4,1024,128]{2,1,0:T(8,128)(2,1)S(1)}, bf16[8,512]{1,0:T(8,128)(2,1)S(1)}) custom-call(s32[56]{0:T(128)S(1)} %get-tuple-element.142.table, bf16[4,2,1024]{2,1,0:T(2,128)(2,1)} %get-tuple-element.143.refs_0_, bf16[4,2,128]{2,1,0:T(2,128)(2,1)} %get-tuple-element.144.refs_1_, ...), custom_call_target="tpu_custom_call" | custom-call | tf_op jit(solution)/shard_map/cond/branch_2_fun/move_attend_7/pallas_call | solution.py:712
  62.3 0.6 reshape.83
  62.9 1.0 %copy.36 = bf16[1,4,1024,1,128]{4,2,3,1,0:T(8,128)(2,1)} copy(bf16[1,4,1024,1,128]{4,2,3,1,0:T(8,128)(2,1)S(1)} %bitcast.22) | data formatting | bytes 2097152
  63.9 1.0 %copy.37 = bf16[1,4,1024,1,128]{4,2,3,1,0:T(8,128)(2,1)} copy(bf16[1,4,1024,1,128]{4,2,3,1,0:T(8,128)(2,1)S(1)} %bitcast.23) | data formatting | bytes 2097152
